TPU v7x, 512 devices: a whole 4x4x16 slice. The times are simulated.
512 devices in a mesh: dp: 2 (over core), fsdp: 16 (over x, y), tensor: 16 (over z).
Axes of the slice: x: 4, y: 4, z: 16, core: 2. Of those that a mesh axis runs over, the one named last changes fastest.
Arguments:
- momentum: bfloat16 [2, 8192, 14336], P('dp', 'fsdp', 'tensor'), may hold values from -40 to 40
- gradient: bfloat16 [2, 8192, 14336], P('dp', 'fsdp', 'tensor'), may hold values from -48 to 48
- right_factor: float32 [14336, 128], P('tensor'), may hold values from -0.046875 to 0.046875
Outputs:
- new_momentum: bfloat16 [2, 8192, 14336], P('dp', 'fsdp', 'tensor')
- update: bfloat16 [8192, 14336], P('fsdp', 'tensor')
- new_factor: float32 [14336, 128], P('tensor')
All inputs are finite; a program needn't handle non-finite values.
Results may differ from a plain program's by a relative error of at most 0.012.
Values may be sent and summed in bfloat16 or wider, within the bound.
A program may use at most 64 MiB of HBM per device.

v0:
```python
import math

import jax
import jax.numpy as jnp
from jax import lax
from jax.sharding import PartitionSpec as P

D = 8192
FF = 14336
RANK = 128
ITERS = 2


def orthonormal(rows, gram):
    lower = jnp.linalg.cholesky(gram)
    return lax.linalg.triangular_solve(
        lower, rows, left_side=False, lower=True, transpose_a=True
    ).astype(jnp.bfloat16)


def shards(momentum, gradient, right_factor):
    buffer = (momentum[0].astype(jnp.float32) + gradient[0].astype(jnp.float32)).astype(
        jnp.bfloat16
    )
    replicas = lax.axis_size("dp")
    factor_b = right_factor.astype(jnp.bfloat16)
    ortho_b = None
    right_b = None
    new_factor = right_factor
    for step in range(ITERS):
        partial_left = jnp.dot(buffer, factor_b, preferred_element_type=jnp.float32)
        left = lax.psum(partial_left, ("dp", "tensor")) / replicas
        gram = lax.psum(jnp.dot(left.T, left, precision=lax.Precision.HIGHEST), "fsdp")
        ortho_b = orthonormal(left, gram)
        partial_right = lax.dot_general(
            buffer, ortho_b, (((0,), (0,)), ((), ())), preferred_element_type=jnp.float32
        )
        right = lax.psum(partial_right, ("dp", "fsdp")) / replicas
        squares = lax.psum(jnp.sum(right * right, axis=0), "tensor")
        new_factor = right / jnp.sqrt(squares + 1e-06)
        factor_b = new_factor.astype(jnp.bfloat16)
        right_b = right.astype(jnp.bfloat16)
    feedback = jnp.dot(ortho_b, right_b.T, preferred_element_type=jnp.float32)
    new_momentum = (buffer.astype(jnp.float32) - 0.05 * feedback).astype(jnp.bfloat16)[None]
    scale_value = math.sqrt(D * FF / RANK)
    update = (
        scale_value * jnp.dot(ortho_b, factor_b.T, preferred_element_type=jnp.float32)
    ).astype(jnp.bfloat16)
    return (new_momentum, update, new_factor)


def solution(mesh):
    placed = (P("dp", "fsdp", "tensor"), P("dp", "fsdp", "tensor"), P("tensor", None))
    return jax.shard_map(
        shards,
        mesh=mesh,
        in_specs=placed,
        out_specs=(P("dp", "fsdp", "tensor"), P("fsdp", "tensor"), P("tensor", None)),
        check_vma=False,
    )
```

profile of v0, /device:TPU:1, one launch (start us, length us, event | category | flops | bytes accessed | tf_op | source)
XLA Modules:
  0.0 1044.2 jit_solution(9465350329947401382)
XLA Ops:
  7.2 0.0 copy-start.4
  7.2 0.0 all-reduce.7.cloned.1.call-start
  7.2 1.7 fusion.3
  8.9 0.0 copy-done.4
  9.0 1.1 fusion.15
  10.1 0.0 all-reduce.7.cloned.1.call-update
  10.1 0.0 all-reduce.9.cloned.1.call-start
  10.1 212.3 %all-reduce.7.cloned.1.call-done = f32[512,128]{1,0:T(8,128)} async-done(((f32[512,128]{1,0:T(8,128)}), f32[512,128]{1,0:T(8,128)}) %all-reduce.7.cloned.1.call-update) | async-done | bytes 262160 | tf_op jit(solution)/shard_map/psum | solution.py:32
  222.4 0.0 copy-start.2
  222.4 2.3 fusion.8
  224.8 0.0 all-reduce.9.cloned.1.call-update
  224.8 0.0 all-reduce.11.cloned.1.call-start
  224.8 111.5 %all-reduce.9.cloned.1.call-done = f32[128,128]{0,1:T(8,128)} async-done(((f32[128,128]{0,1:T(8,128)}), f32[128,128]{0,1:T(8,128)}) %all-reduce.9.cloned.1.call-update) | async-done | bytes 65552 | tf_op jit(solution)/shard_map/psum | solution.py:33
  336.3 0.9 copy.7
  337.3 0.9 fusion.26
  338.1 11.7 %cholesky.44 = f32[128,128]{1,0:T(8,128)S(1)} custom-call(f32[128,128]{1,0:T(8,128)S(1)} %fusion.26), custom_call_target="Cholesky" | custom-call | tf_op jit(solution)/shard_map/jit(cholesky)/cholesky | solution.py:15
  349.9 0.6 compare_reduce_fusion.1
  350.5 0.7 fusion.21
  351.2 9.8 custom-call.6
  361.0 0.0 copy-done.2
  361.0 0.4 fusion.1
  361.4 1.2 fusion.35
  362.6 0.0 all-reduce.11.cloned.1.call-update
  362.7 0.0 all-reduce.13.cloned.1.call-start
  362.7 134.6 %all-reduce.11.cloned.1.call-done = f32[896,128]{1,0:T(8,128)} async-done(((f32[896,128]{1,0:T(8,128)}), f32[896,128]{1,0:T(8,128)}) %all-reduce.11.cloned.1.call-update) | async-done | bytes 458768 | tf_op jit(solution)/shard_map/psum | solution.py:38
  497.3 1.2 multiply_reduce_fusion.1
  498.5 24.8 %psum.59 = f32[128]{0:T(128)S(1)} all-reduce(f32[128]{0:T(128)S(1)} %multiply_reduce_fusion.1), channel_id=1, replica_groups=mesh['dp'=2,'fsdp'=16,'tensor'=16] {'tensor'}, use_global_device_ids=true, to_apply=%region_6.9 | all-reduce | flops 128 | bytes 1024 | tf_op jit(solution)/shard_map/psum | solution.py:39
  523.3 2.1 fusion.10
  525.5 0.0 all-reduce.13.cloned.1.call-update
  525.5 0.0 all-reduce.15.cloned.1.call-start
  525.5 207.6 %all-reduce.13.cloned.1.call-done = f32[512,128]{1,0:T(8,128)} async-done(((f32[512,128]{1,0:T(8,128)}), f32[512,128]{1,0:T(8,128)}) %all-reduce.13.cloned.1.call-update) | async-done | bytes 262160 | tf_op jit(solution)/shard_map/psum | solution.py:32
  733.1 0.0 copy-start.3
  733.1 2.3 fusion.5
  735.5 0.0 all-reduce.15.cloned.1.call-update
  735.5 0.2 all-reduce.17.cloned.1.call-start
  735.7 110.9 %all-reduce.15.cloned.1.call-done = f32[128,128]{0,1:T(8,128)} async-done(((f32[128,128]{0,1:T(8,128)}), f32[128,128]{0,1:T(8,128)}) %all-reduce.15.cloned.1.call-update) | async-done | bytes 65552 | tf_op jit(solution)/shard_map/psum | solution.py:33
  846.6 0.9 copy.9
  847.5 0.9 fusion.24
  848.4 11.7 %cholesky.55 = f32[128,128]{1,0:T(8,128)S(1)} custom-call(f32[128,128]{1,0:T(8,128)S(1)} %fusion.24), custom_call_target="Cholesky" | custom-call | tf_op jit(solution)/shard_map/jit(cholesky)/cholesky | solution.py:15
  860.1 0.6 compare_reduce_fusion
  860.8 0.7 fusion.22
  861.4 9.8 custom-call.7
  871.2 0.0 copy-done.3
  871.2 0.4 fusion.2
  871.7 1.2 fusion.36
  872.9 0.0 all-reduce.17.cloned.1.call-update
  872.9 134.6 %all-reduce.17.cloned.1.call-done = f32[896,128]{1,0:T(8,128)} async-done(((f32[896,128]{1,0:T(8,128)}), f32[896,128]{1,0:T(8,128)}) %all-reduce.17.cloned.1.call-update) | async-done | bytes 458768 | tf_op jit(solution)/shard_map/psum | solution.py:38
  1007.5 1.2 multiply_reduce_fusion
  1008.7 24.8 %psum.63 = f32[128]{0:T(128)S(1)} all-reduce(f32[128]{0:T(128)S(1)} %multiply_reduce_fusion), channel_id=1, replica_groups=mesh['dp'=2,'fsdp'=16,'tensor'=16] {'tensor'}, use_global_device_ids=true, to_apply=%region_11.14 | all-reduce | flops 128 | bytes 1024 | tf_op jit(solution)/shard_map/psum | solution.py:39
  1033.5 1.1 multiply_divide_fusion
  1034.6 0.0 copy-start.1
  1034.6 0.0 copy-start
  1034.6 1.4 multiply_convert_fusion
  1036.0 0.0 copy-done
  1036.0 1.4 fusion
  1037.3 0.0 copy-done.1
  (4 shorter events, 0.1 us)
Async XLA Ops:
  7.2 1.8 copy-start.4
  7.2 215.3 %all-reduce.7.cloned.1.call-start = ((), (), s32[]{:S(2)}) async-start(), calls=%async_computation | async-start | bytes 524288 | tf_op jit(solution)/shard_map/psum | solution.py:32
  10.1 326.3 %all-reduce.9.cloned.1.call-start = ((), (), s32[]{:S(2)}) async-start(), calls=%async_computation.1 | async-start | bytes 131072 | tf_op jit(solution)/shard_map/psum | solution.py:33
  222.4 138.6 %copy-start.2 = (f32[512,128]{1,0:T(8,128)S(1)}, f32[512,128]{1,0:T(8,128)}, u32[]{:S(2)}) copy-start(f32[512,128]{1,0:T(8,128)} %all-reduce.7.cloned.1.call-done) | copy-start | bytes 786436
  224.8 272.5 %all-reduce.11.cloned.1.call-start = ((), (), s32[]{:S(2)}) async-start(), calls=%async_computation.2 | async-start | bytes 917504 | tf_op jit(solution)/shard_map/psum | solution.py:38
  362.7 370.4 %all-reduce.13.cloned.1.call-start = ((), (), s32[]{:S(2)}) async-start(), calls=%async_computation.3 | async-start | bytes 524288 | tf_op jit(solution)/shard_map/psum | solution.py:32
  525.5 321.1 %all-reduce.15.cloned.1.call-start = ((), (), s32[]{:S(2)}) async-start(), calls=%async_computation.4 | async-start | bytes 131072 | tf_op jit(solution)/shard_map/psum | solution.py:33
  733.1 138.1 %copy-start.3 = (f32[512,128]{1,0:T(8,128)S(1)}, f32[512,128]{1,0:T(8,128)}, u32[]{:S(2)}) copy-start(f32[512,128]{1,0:T(8,128)} %all-reduce.13.cloned.1.call-done) | copy-start | bytes 786436
  735.5 272.1 %all-reduce.17.cloned.1.call-start = ((), (), s32[]{:S(2)}) async-start(), calls=%async_computation.5 | async-start | bytes 917504 | tf_op jit(solution)/shard_map/psum | solution.py:38
  1034.6 2.7 copy-start.1
  1034.6 1.4 copy-start
Sparse Core Ops, SparseCore 0:
  10.9 211.5 all-reduce.6
  226.5 109.7 all-reduce.8
  362.8 134.4 all-reduce.10
  525.6 207.4 all-reduce.12
  736.7 109.7 all-reduce.14
  873.0 134.4 all-reduce.16
where the time goes:
time: 1050 us; the launch traced here: 1040 us
  waiting for transfers between devices  912 us (87%)
  other arithmetic  52.5 us (5%)
  blocking collectives  49.7 us (5%)
  between operations  14.2 us (1%)
  matrix products  13.9 us (1%)
    psum x2, waiting for transfers between devices, shards(): left = lax.psum(partial_left, ('dp', 'tensor')) / replicas  420 us
    psum x2, waiting for transfers between devices, shards(): right = lax.psum(partial_right, ('dp', 'fsdp')) / replicas  269 us
    psum x2, waiting for transfers between devices, shards(): lax.psum(jnp.dot(left.T, left, precision=lax.Precision.HIGHEST), 'fsdp')  222 us
    psum x2, blocking collectives, shards(): squares = lax.psum(jnp.sum(right * right, axis=0), 'tensor')  49.7 us
    another operation x6, other arithmetic, orthonormal(): lower = jnp.linalg.cholesky(gram)  24.8 us
  transfers between devices with their start and end apart: 6, of which 6 were waited for; matrix products, arithmetic and copies ran while one was open for 0% of the time, Pallas kernels for 0%

commit v1 on v0

v1 whole, which is shorter than its diff:
```python
import math

import jax
import jax.numpy as jnp
from jax import lax
from jax.experimental import pallas as pl
from jax.experimental.pallas import tpu as pltpu
from jax.sharding import PartitionSpec as P

D = 8192
FF = 14336
RANK = 128
MESH = pl.DeviceIdType.MESH
F32 = jnp.float32
BF16 = jnp.bfloat16
HIGHEST = lax.Precision.HIGHEST

NZ = 16
NXY = 16
GROUP = 32
ROWS = 512
HALF = 256
COLS = 896
XCH = HALF // NZ
WCH = 32
WOWN = COLS // WCH
TILES = COLS // 128
GCH = 8
NB = 16


def ring_offsets():
    return sorted(range(1, NZ), key=lambda d: -min(d, NZ - d))


def group_offsets():
    offs = [(dc, dx, dy) for dc in range(2) for dx in range(4) for dy in range(4)]
    offs.remove((0, 0, 0))
    return sorted(offs, key=lambda o: -(min(o[1], 4 - o[1]) + min(o[2], 4 - o[2])))


def split3(a):
    high = a.astype(BF16)
    rest = a - high.astype(F32)
    mid = rest.astype(BF16)
    low = (rest - mid.astype(F32)).astype(BF16)
    return high, mid, low


def outer_f32(u, v):
    u1, u2, u3 = split3(u)
    v1, v2, v3 = split3(v)
    left = jnp.concatenate([u1, u1, u2, u1, u2, u3], 0)
    right = jnp.concatenate([v1, v2, v1, v3, v2, v1], 0)
    return lax.dot_general(left, right, (((0,), (0,)), ((), ())), preferred_element_type=F32)


def inverse_cholesky(a_ref, e_ref):
    rows = lax.broadcasted_iota(jnp.int32, (RANK, RANK), 0)
    cols = lax.broadcasted_iota(jnp.int32, (RANK, RANK), 1)
    e_ref[...] = jnp.where(rows == cols, 1.0, 0.0).astype(F32)
    sub = lax.broadcasted_iota(jnp.int32, (NB, RANK), 0)

    def spread(t, j):
        return jnp.broadcast_to(t[j : j + 1, :], (NB, RANK))

    for base in range(0, RANK, NB):
        xa = a_ref[base : base + NB, :]
        xe = e_ref[base : base + NB, :]
        col = [
            jnp.broadcast_to(xa[:, base + k : base + k + 1], (NB, RANK)) for k in range(NB)
        ]
        va, ve, out = [], [], []
        for j in range(NB):
            pivot = spread(col[j], j)
            inv = 1.0 / pivot
            row_e = spread(xe, j)
            out.append((row_e * lax.rsqrt(pivot))[0:1])
            row_a = inv * spread(xa, j)
            row_e = inv * row_e
            va.append(row_a[0:1])
            ve.append(row_e[0:1])
            if j + 1 < NB:
                below = jnp.where(sub > j, col[j], 0.0)
                xa = xa - below * row_a
                xe = xe - below * row_e
                for k in range(j + 1, NB):
                    col[k] = col[k] - below * (inv * spread(col[k], j))
        last = base + NB
        if last < RANK:
            v = jnp.concatenate([jnp.concatenate(va, 0), jnp.concatenate(ve, 0)], 1)
            change = outer_f32(xa, v)
            a_ref[last:, :] = a_ref[last:, :] - change[last:, :RANK]
            e_ref[last:, :] = e_ref[last:, :] - change[last:, RANK:]
        e_ref[base:last, :] = jnp.concatenate(out, 0)


def right_times(tiles_ref, m):
    parts = jnp.concatenate(split3(m), 0)
    out = []
    for i in range(TILES):
        tile = tiles_ref[i * 128 : (i + 1) * 128, :]
        r = lax.dot_general(tile, parts, (((0,), (1,)), ((), ())), preferred_element_type=F32)
        out.append(r[:, :RANK] + (r[:, RANK : 2 * RANK] + r[:, 2 * RANK :]))
    return out


def rows_times(x, m):
    r = lax.dot_general(
        x, jnp.concatenate(split3(m), 0), (((1,), (1,)), ((), ())), preferred_element_type=F32
    )
    return r[:, :RANK] + (r[:, RANK : 2 * RANK] + r[:, 2 * RANK :])


def kernel(
    mom, grad, fac, new_mom, update, new_fac,
    m_v, g_v, f_v, fb, own, oth, xs, xr, xo, xa, xoth, ws, wr, wo, wa, gs, gr, go, ga,
    qs, qr, lower, a_s, right, ob, nm_v, up_v, nf_v, load, send, recv, store,
):
    c = lax.axis_index("dp")
    f = lax.axis_index("fsdp")
    t = lax.axis_index("tensor")
    x = f // 4
    y = lax.rem(f, 4)
    me = f * 2 + c
    other = 1 - c
    ring = [(c, f, lax.rem(t + d, NZ)) for d in ring_offsets()]
    group = []
    for dc, dx, dy in group_offsets():
        qf = lax.rem(x + dx, 4) * 4 + lax.rem(y + dy, 4)
        group.append((c if dc == 0 else other, qf, t))
    partner = (other, f, t)
    owner_w = me < WOWN
    owner_g = c == lax.rem(f, 2)

    def put(src, dst, phase, to):
        pltpu.make_async_remote_copy(
            src_ref=src, dst_ref=dst, send_sem=send.at[phase], recv_sem=recv.at[phase],
            device_id=to, device_id_type=MESH,
        ).start()

    def got(region, phase):
        pltpu.make_async_remote_copy(
            src_ref=region, dst_ref=region, send_sem=send.at[phase], recv_sem=recv.at[phase],
            device_id=partner, device_id_type=MESH,
        ).wait_recv()

    def sent(region, phase):
        pltpu.make_async_remote_copy(
            src_ref=region, dst_ref=region, send_sem=send.at[phase], recv_sem=recv.at[phase],
            device_id=partner, device_id_type=MESH,
        ).wait_send()

    barrier = pltpu.get_barrier_semaphore()
    for to in ring + group:
        pl.semaphore_signal(barrier, inc=1, device_id=to, device_id_type=MESH)

    starts = [pl.multiple_of(lax.rem(other * HALF + 128 * i, ROWS), 128) for i in range(4)]
    loads = []
    for i in range(4):
        r = pl.ds(starts[i], 128)
        pair = [
            pltpu.make_async_copy(mom.at[0, r], m_v.at[r], load.at[2 * i]),
            pltpu.make_async_copy(grad.at[0, r], g_v.at[r], load.at[2 * i + 1]),
        ]
        for copy in pair:
            copy.start()
        loads.append(pair)
    load_f = pltpu.make_async_copy(fac, f_v, load.at[8])
    load_f.start()
    for i in range(4):
        for copy in loads[i]:
            copy.wait()
        r = pl.ds(starts[i], 128)
        own[r, :] = (m_v[r, :].astype(F32) + g_v[r, :].astype(F32)).astype(BF16)
    load_f.wait()
    fb[...] = f_v[...].astype(BF16)

    mine = pl.ds(pl.multiple_of(c * HALF, HALF), HALF)
    theirs = pl.ds(pl.multiple_of(other * HALF, HALF), HALF)
    pl.semaphore_wait(barrier, len(ring) + len(group))

    put(own.at[theirs], oth, 0, partner)

    def left_out(it, acc):
        base = 2 + 7 * it
        xs[it] = (0.5 * acc).astype(BF16)
        for to in ring:
            src = xs.at[it, pl.ds(pl.multiple_of(to[2] * XCH, XCH), XCH)]
            put(src, xr.at[it, pl.ds(pl.multiple_of(t * XCH, XCH), XCH)], base, to)
        rows = pl.ds(pl.multiple_of(t * XCH, XCH), XCH)
        xr[it, rows, :] = xs[it, rows, :]

    def left_owned(it):
        got(xr.at[it, pl.ds(0, HALF - XCH)], 2 + 7 * it)
        total = xr[it, 0:XCH, :].astype(F32)
        for k in range(1, NZ):
            total = total + xr[it, k * XCH : (k + 1) * XCH, :].astype(F32)
        return total

    def left_spread(it, total):
        rows = pl.ds(pl.multiple_of(t * XCH, XCH), XCH)
        xo[it] = total.astype(BF16)
        for to in ring:
            put(xo.at[it], xa.at[it, rows], 3 + 7 * it, to)
        xa[it, rows, :] = total.astype(BF16)

    def left_here(it):
        got(xa.at[it, pl.ds(0, HALF - XCH)], 3 + 7 * it)
        return xa[it]

    def right_out(it, left):
        base = 4 + 7 * it
        dims = (((0,), (0,)), ((), ()))
        part = lax.dot_general(left, own[mine, :], dims, preferred_element_type=F32)
        part = part + lax.dot_general(left, oth[...], dims, preferred_element_type=F32)
        part = (0.5 * part).astype(BF16)
        for i in range(TILES):
            ws[it, i * 128 : (i + 1) * 128, :] = part[:, i * 128 : (i + 1) * 128]
        dst = wr.at[it, pl.ds(pl.multiple_of(me * WCH, WCH), WCH)]
        for to in group:
            q = to[1] * 2 + to[0]

            @pl.when(q < WOWN)
            def _():
                put(ws.at[it, pl.ds(pl.multiple_of(q * WCH, WCH), WCH)], dst, base, to)

        @pl.when(owner_w)
        def _():
            rows = pl.ds(pl.multiple_of(me * WCH, WCH), WCH)
            wr[it, rows, :] = ws[it, rows, :]

    def right_spread(it):
        @pl.when(owner_w)
        def _():
            got(wr.at[it, pl.ds(0, (GROUP - 1) * WCH)], 4 + 7 * it)
            total = wr[it, 0:WCH, :].astype(F32)
            for k in range(1, GROUP):
                total = total + wr[it, k * WCH : (k + 1) * WCH, :].astype(F32)
            wo[it] = total.astype(BF16)
            rows = pl.ds(pl.multiple_of(me * WCH, WCH), WCH)
            for to in group:
                put(wo.at[it], wa.at[it, rows], 5 + 7 * it, to)
            wa[it, rows, :] = total.astype(BF16)

    def right_here(it):
        @pl.when(owner_w)
        def _():
            got(wa.at[it, pl.ds(0, (WOWN - 1) * WCH)], 5 + 7 * it)

        @pl.when(jnp.logical_not(owner_w))
        def _():
            got(wa.at[it, pl.ds(0, WOWN * WCH)], 5 + 7 * it)

    def gram_out(it, left):
        dims = (((0,), (0,)), ((), ()))
        gs[it] = lax.dot_general(left, left, dims, preferred_element_type=F32)
        dst = gr.at[it, pl.ds(pl.multiple_of(me * GCH, GCH), GCH)]
        for to in group:

            @pl.when(to[0] == lax.rem(to[1], 2))
            def _():
                rows = pl.ds(pl.multiple_of(to[1] * GCH, GCH), GCH)
                put(gs.at[it, rows], dst, 6 + 7 * it, to)

        @pl.when(owner_g)
        def _():
            rows = pl.ds(pl.multiple_of(f * GCH, GCH), GCH)
            gr[it, pl.ds(pl.multiple_of(me * GCH, GCH), GCH), :] = gs[it, rows, :]

    def gram_spread(it):
        @pl.when(owner_g)
        def _():
            got(gr.at[it, pl.ds(0, (GROUP - 1) * GCH)], 6 + 7 * it)
            total = gr[it, 0:GCH, :]
            for k in range(1, GROUP):
                total = total + gr[it, k * GCH : (k + 1) * GCH, :]
            go[it] = total
            rows = pl.ds(pl.multiple_of(f * GCH, GCH), GCH)
            for to in group:
                put(go.at[it], ga.at[it, rows], 7 + 7 * it, to)
            ga[it, rows, :] = total

    def gram_here(it):
        @pl.when(owner_g)
        def _():
            got(ga.at[it, pl.ds(0, RANK - GCH)], 7 + 7 * it)

        @pl.when(jnp.logical_not(owner_g))
        def _():
            got(ga.at[it], 7 + 7 * it)

        return ga[it]

    def squares_out(it, tiles):
        total = jnp.sum(tiles[0] * tiles[0], axis=0, keepdims=True)
        for tile in tiles[1:]:
            total = total + jnp.sum(tile * tile, axis=0, keepdims=True)
        qs[it] = jnp.broadcast_to(total, (8, RANK))
        rows = pl.ds(pl.multiple_of(t * 8, 8), 8)
        for to in ring:
            put(qs.at[it], qr.at[it, rows], 8 + 7 * it, to)
        qr[it, rows, :] = qs[it]

    def norms(it):
        got(qr.at[it, pl.ds(0, (NZ - 1) * 8)], 8 + 7 * it)
        total = qr[it, 0:8, :]
        for k in range(1, NZ):
            total = total + qr[it, k * 8 : (k + 1) * 8, :]
        return jnp.sqrt(total[0:1, :] + 1e-06)

    part = jnp.dot(own[mine, :], fb[...], preferred_element_type=F32)
    got(oth, 0)
    left_out(0, part + jnp.dot(oth[...], fb[...], preferred_element_type=F32))
    left_spread(0, left_owned(0))
    left = left_here(0)
    right_out(0, left)
    gram_out(0, left)
    right_spread(0)
    gram_spread(0)
    right_here(0)

    factor_t = jnp.concatenate([wa[0, i * 128 : (i + 1) * 128, :] for i in range(TILES)], 1)
    nt = (((1,), (1,)), ((), ()))
    part = lax.dot_general(own[mine, :], factor_t, nt, preferred_element_type=F32)
    left_out(1, part + lax.dot_general(oth[...], factor_t, nt, preferred_element_type=F32))
    a_s[...] = gram_here(0)
    inverse_cholesky(a_s, lower.at[0])
    owned = left_owned(1)
    left_spread(
        1,
        lax.dot_general(owned, lower[0], nt, preferred_element_type=F32, precision=HIGHEST),
    )
    squares_out(0, right_times(wa.at[0], lower[0]))
    left = left_here(1)
    gram_out(1, left)
    right_out(1, left)
    put(xa.at[1], xoth, 1, partner)
    gram_spread(1)
    right_spread(1)
    scale = jnp.broadcast_to(1.0 / norms(0), (RANK, RANK))
    a_s[...] = gram_here(1) * scale * scale.T
    inverse_cholesky(a_s, lower.at[1])
    mix = lower[1] * scale
    got(xoth, 1)
    ob[mine, :] = rows_times(left, mix).astype(BF16)
    ob[theirs, :] = rows_times(xoth[...], mix).astype(BF16)
    right_here(1)
    tiles = right_times(wa.at[1], mix)
    squares_out(1, tiles)
    for i in range(TILES):
        right[i * 128 : (i + 1) * 128, :] = tiles[i]
    right_b = right[...].astype(BF16)
    outs = []
    for i in range(4):
        r = pl.ds(i * 128, 128)
        feedback = lax.dot_general(ob[r, :], right_b, nt, preferred_element_type=F32)
        nm_v[r, :] = (own[r, :].astype(F32) - 0.05 * feedback).astype(BF16)
        copy = pltpu.make_async_copy(nm_v.at[r], new_mom.at[0, r], store.at[i])
        copy.start()
        outs.append(copy)
    nf_v[...] = right[...] * (1.0 / norms(1))
    copy = pltpu.make_async_copy(nf_v, new_fac, store.at[8])
    copy.start()
    outs.append(copy)
    factor_b = nf_v[...].astype(BF16)
    for i in range(4):
        r = pl.ds(i * 128, 128)
        low_rank = lax.dot_general(ob[r, :], factor_b, nt, preferred_element_type=F32)
        up_v[r, :] = (math.sqrt(D * FF / RANK) * low_rank).astype(BF16)
        copy = pltpu.make_async_copy(up_v.at[r], update.at[r], store.at[4 + i])
        copy.start()
        outs.append(copy)

    sent(oth, 0)
    sent(xoth, 1)
    for it in range(2):
        sent(xs.at[it, pl.ds(0, HALF - XCH)], 2 + 7 * it)
        sent(xa.at[it, pl.ds(0, HALF - XCH)], 3 + 7 * it)

        @pl.when(owner_w)
        def _():
            sent(ws.at[it, pl.ds(0, (WOWN - 1) * WCH)], 4 + 7 * it)
            sent(wr.at[it, pl.ds(0, (GROUP - 1) * WCH)], 5 + 7 * it)

        @pl.when(jnp.logical_not(owner_w))
        def _():
            sent(ws.at[it, pl.ds(0, WOWN * WCH)], 4 + 7 * it)

        @pl.when(owner_g)
        def _():
            sent(gs.at[it, pl.ds(0, RANK - GCH)], 6 + 7 * it)
            sent(gr.at[it, pl.ds(0, (GROUP - 1) * GCH)], 7 + 7 * it)

        @pl.when(jnp.logical_not(owner_g))
        def _():
            sent(gs.at[it], 6 + 7 * it)

        sent(qr.at[it, pl.ds(0, (NZ - 1) * 8)], 8 + 7 * it)
    for copy in outs:
        copy.wait()


def shards(momentum, gradient, right_factor):
    scratch = [
        pltpu.VMEM((ROWS, COLS), BF16),
        pltpu.VMEM((ROWS, COLS), BF16),
        pltpu.VMEM((COLS, RANK), F32),
        pltpu.VMEM((COLS, RANK), BF16),
        pltpu.VMEM((ROWS, COLS), BF16),
        pltpu.VMEM((HALF, COLS), BF16),
        pltpu.VMEM((2, HALF, RANK), BF16),
        pltpu.VMEM((2, HALF, RANK), BF16),
        pltpu.VMEM((2, XCH, RANK), BF16),
        pltpu.VMEM((2, HALF, RANK), BF16),
        pltpu.VMEM((HALF, RANK), BF16),
        pltpu.VMEM((2, COLS, RANK), BF16),
        pltpu.VMEM((2, GROUP * WCH, RANK), BF16),
        pltpu.VMEM((2, WCH, RANK), BF16),
        pltpu.VMEM((2, COLS, RANK), BF16),
        pltpu.VMEM((2, RANK, RANK), F32),
        pltpu.VMEM((2, GROUP * GCH, RANK), F32),
        pltpu.VMEM((2, GCH, RANK), F32),
        pltpu.VMEM((2, RANK, RANK), F32),
        pltpu.VMEM((2, 8, RANK), F32),
        pltpu.VMEM((2, NZ * 8, RANK), F32),
        pltpu.VMEM((2, RANK, RANK), F32),
        pltpu.VMEM((RANK, RANK), F32),
        pltpu.VMEM((COLS, RANK), F32),
        pltpu.VMEM((ROWS, RANK), BF16),
        pltpu.VMEM((ROWS, COLS), BF16),
        pltpu.VMEM((ROWS, COLS), BF16),
        pltpu.VMEM((COLS, RANK), F32),
        pltpu.SemaphoreType.DMA((9,)),
        pltpu.SemaphoreType.DMA((16,)),
        pltpu.SemaphoreType.DMA((16,)),
        pltpu.SemaphoreType.DMA((9,)),
    ]
    anywhere = pl.BlockSpec(memory_space=pl.ANY)
    return pl.pallas_call(
        kernel,
        out_shape=(
            jax.ShapeDtypeStruct((1, ROWS, COLS), BF16),
            jax.ShapeDtypeStruct((ROWS, COLS), BF16),
            jax.ShapeDtypeStruct((COLS, RANK), F32),
        ),
        in_specs=[anywhere] * 3,
        out_specs=(anywhere,) * 3,
        scratch_shapes=scratch,
        compiler_params=pltpu.CompilerParams(
            collective_id=0, has_side_effects=True, vmem_limit_bytes=60 * 2**20
        ),
        cost_estimate=pl.CostEstimate(
            flops=12 * ROWS * COLS * RANK, bytes_accessed=6 * 2**20, transcendentals=0
        ),
    )(momentum, gradient, right_factor)


def solution(mesh):
    placed = (P("dp", "fsdp", "tensor"), P("dp", "fsdp", "tensor"), P("tensor", None))
    return jax.shard_map(
        shards,
        mesh=mesh,
        in_specs=placed,
        out_specs=(P("dp", "fsdp", "tensor"), P("fsdp", "tensor"), P("tensor", None)),
        check_vma=False,
    )
```

time: 1050 us -> 87.7 us (0.08)
  waiting for transfers between devices: 912 us -> 0 us
  Pallas kernels: 0 us -> 82.5 us
  other arithmetic: 52.5 us -> 0 us
  blocking collectives: 49.7 us -> 0 us
  matrix products: 13.9 us -> 0 us
  between operations: 14.2 us -> 0.65 us
    psum x6 -> x0, waiting for transfers between devices: 912 us -> none  [the longest x2 420 us: shards(): left = lax.psum(partial_left, ('dp', 'tensor')) / replicas]
    pallas_call x0 -> x1, Pallas kernels: none -> 82.5 us  [shards(): pl.pallas_call(kernel, out_shape=(jax.ShapeDtypeStruct((1, ROWS, COLS), B...]
    psum x2 -> x0, blocking collectives: 49.7 us -> none  [shards(): squares = lax.psum(jnp.sum(right * right, axis=0), 'tensor')]
    another operation x10 -> x0, other arithmetic: 45.7 us -> none  [the longest x6 24.8 us: orthonormal(): lower = jnp.linalg.cholesky(gram)]
    dot_general x8 -> x0, matrix products: 13 us -> none  [the longest x2 4.65 us: shards(): jnp.dot(left.T, left, precision=lax.Precision.HIGHEST)]
  transfers between devices with their start and end apart: 6 -> 0, of which waited for: 6 -> 0; matrix products, arithmetic and copies ran while one was open for 0% -> 0% of each run, Pallas kernels for 0% -> 0%
where the time goes in v1:
time: 87.7 us; the launch traced here: 87.5 us
  Pallas kernels  82.5 us (94%)
  local copies, waits for them, and re-layouts  4.35 us (5%)
    pallas_call x1, Pallas kernels, shards(): pl.pallas_call(kernel, out_shape=(jax.ShapeDtypeStruct((1, ROWS, COLS), B...  82.5 us
    unnamed x7, local copies, waits for them, and re-layouts  4.35 us

profile of v1, /device:TPU:1, one launch (start us, length us, event | category | flops | bytes accessed | tf_op | source)
XLA Modules:
  0.0 87.5 jit_solution(11643075719080125313)
XLA Ops:
  0.6 82.5 %shard_map.58 = (bf16[1,512,896]{2,1,0:T(8,128)(2,1)}, bf16[512,896]{1,0:T(8,128)(2,1)}, f32[896,128]{1,0:T(8,128)}) custom-call(bf16[1,512,896]{2,1,0:T(8,128)(2,1)} %mom.1, bf16[1,512,896]{2,1,0:T(8,128)(2,1)} %grad.1, f32[896,128]{1,0:T(8,128)} %fac.1), custom_call_target="tpu_custom_call" | custom-call | flops 704643072 | bytes 6291456 | tf_op jit(solution)/shard_map/pallas_call | solution.py:440
  83.1 0.0 copy-start
  83.1 2.3 %copy.9 = bf16[1,512,896]{2,1,0:T(8,128)(2,1)} copy(bf16[1,512,896]{2,1,0:T(8,128)(2,1)} %get-tuple-element.6) | data formatting | bytes 1835008
  85.4 0.0 copy-done
  85.4 0.0 copy-start.1
  85.4 0.9 %copy.10 = bf16[512,896]{1,0:T(8,128)(2,1)} copy(bf16[512,896]{1,0:T(8,128)(2,1)S(1)} %copy-done) | data formatting | bytes 1835008
  86.3 0.4 copy-done.1
  86.7 0.8 copy.11
Async XLA Ops:
  83.1 2.3 %copy-start = (bf16[512,896]{1,0:T(8,128)(2,1)S(1)}, bf16[512,896]{1,0:T(8,128)(2,1)}, u32[]{:S(2)}) copy-start(bf16[512,896]{1,0:T(8,128)(2,1)} %get-tuple-element.7) | copy-start | bytes 2752516
  85.4 1.3 %copy-start.1 = (f32[896,128]{1,0:T(8,128)S(1)}, f32[896,128]{1,0:T(8,128)}, u32[]{:S(2)}) copy-start(f32[896,128]{1,0:T(8,128)} %get-tuple-element.8) | copy-start | bytes 1376260

commit v2 on v1

v2 whole, which is shorter than its diff:
```python
import math

import jax
import jax.numpy as jnp
from jax import lax
from jax.experimental import pallas as pl
from jax.experimental.pallas import tpu as pltpu
from jax.sharding import PartitionSpec as P

D = 8192
FF = 14336
RANK = 128
MESH = pl.DeviceIdType.MESH
F32 = jnp.float32
BF16 = jnp.bfloat16
HIGHEST = lax.Precision.HIGHEST

NZ = 16
ROWS = 512
HALF = 256
COLS = 896
XCH = 32
WCH = 64
GCH = 8
TILES = COLS // 128
PLACES = COLS // WCH
NB = 16

NEAR_Z = [4, 3, -3, 2, -2, 1, -1]
FAR_Z = sorted(range(1, NZ), key=lambda d: -min(d, NZ - d))
NEAR_XY = [(1, 1), (1, 3), (0, 2), (1, 0), (3, 0), (0, 1), (0, 3), (0, 0)]
FAR_XY = sorted(
    [(dx, dy) for dx in range(4) for dy in range(4) if (dx, dy) != (0, 0)],
    key=lambda o: -(min(o[0], 4 - o[0]) + min(o[1], 4 - o[1])),
)


def split3(a):
    high = a.astype(BF16)
    rest = a - high.astype(F32)
    mid = rest.astype(BF16)
    low = (rest - mid.astype(F32)).astype(BF16)
    return high, mid, low


def outer_f32(u, v):
    u1, u2, u3 = split3(u)
    v1, v2, v3 = split3(v)
    left = jnp.concatenate([u1, u1, u2, u1, u2, u3], 0)
    right = jnp.concatenate([v1, v2, v1, v3, v2, v1], 0)
    return lax.dot_general(left, right, (((0,), (0,)), ((), ())), preferred_element_type=F32)


def inverse_cholesky(a_ref, e_ref, panels):
    if panels[0] == 0:
        rows = lax.broadcasted_iota(jnp.int32, (RANK, RANK), 0)
        cols = lax.broadcasted_iota(jnp.int32, (RANK, RANK), 1)
        e_ref[...] = jnp.where(rows == cols, 1.0, 0.0).astype(F32)
    sub = lax.broadcasted_iota(jnp.int32, (NB, RANK), 0)

    def spread(t, j):
        return jnp.broadcast_to(t[j : j + 1, :], (NB, RANK))

    for base in [p * NB for p in panels]:
        xa = a_ref[base : base + NB, :]
        xe = e_ref[base : base + NB, :]
        col = [
            jnp.broadcast_to(xa[:, base + k : base + k + 1], (NB, RANK)) for k in range(NB)
        ]
        va, ve, out = [], [], []
        for j in range(NB):
            pivot = spread(col[j], j)
            inv = 1.0 / pivot
            row_e = spread(xe, j)
            out.append((row_e * lax.rsqrt(pivot))[0:1])
            row_a = inv * spread(xa, j)
            row_e = inv * row_e
            va.append(row_a[0:1])
            ve.append(row_e[0:1])
            if j + 1 < NB:
                below = jnp.where(sub > j, col[j], 0.0)
                xa = xa - below * row_a
                xe = xe - below * row_e
                for k in range(j + 1, NB):
                    col[k] = col[k] - below * (inv * spread(col[k], j))
        last = base + NB
        if last < RANK:
            v = jnp.concatenate([jnp.concatenate(va, 0), jnp.concatenate(ve, 0)], 1)
            change = outer_f32(xa, v)
            a_ref[last:, :] = a_ref[last:, :] - change[last:, :RANK]
            e_ref[last:, :] = e_ref[last:, :] - change[last:, RANK:]
        e_ref[base:last, :] = jnp.concatenate(out, 0)


def right_times(tiles_ref, m):
    parts = jnp.concatenate(split3(m), 0)
    out = []
    for i in range(TILES):
        tile = tiles_ref[i * 128 : (i + 1) * 128, :]
        r = lax.dot_general(tile, parts, (((0,), (1,)), ((), ())), preferred_element_type=F32)
        out.append(r[:, :RANK] + (r[:, RANK : 2 * RANK] + r[:, 2 * RANK :]))
    return out


def rows_times(x, m):
    r = lax.dot_general(
        x, jnp.concatenate(split3(m), 0), (((1,), (1,)), ((), ())), preferred_element_type=F32
    )
    return r[:, :RANK] + (r[:, RANK : 2 * RANK] + r[:, 2 * RANK :])


def kernel(
    mom, grad, fac, new_mom, update, new_fac,
    m_v, g_v, f_v, fb, own, oth, xs0, xr0, xs1, xr1, xo, xp, xl, xoth, ws, wr, wo, wp, wa, gs, gr, go, gp,
    qs, qr, lower, a_s, right, ob, acc, load, send, recv,
):
    c = lax.axis_index("dp")
    f = lax.axis_index("fsdp")
    t = lax.axis_index("tensor")
    x = f // 4
    y = lax.rem(f, 4)
    other = 1 - c
    partner = (other, f, t)

    def core(dc):
        return c if dc == 0 else other

    def along_z(d, dc=0):
        return (core(dc), f, lax.rem(t + d + NZ, NZ))

    def along_xy(dx, dy, dc=0):
        return (core(dc), lax.rem(x + dx, 4) * 4 + lax.rem(y + dy, 4), t)

    def pair_of(chip):
        px = chip // 4
        return lax.rem(px, 2) * 4 + lax.rem(lax.rem(chip, 4) + 2 * (px // 2), 4)

    pair = pair_of(f)
    half = x // 2
    place = c * 8 + pair
    owner = place < PLACES
    idle = jnp.logical_not(owner)
    ring = [along_z(d) for d in FAR_Z]
    chips = [along_xy(*o) for o in FAR_XY]
    near = [(2 * (len(NEAR_XY) - 1 - i) + dc, along_xy(*o, dc)) for i, o in enumerate(NEAR_XY) for dc in (0, 1)]
    near = [(slot, to) for slot, to in near if slot]

    def chunk(index, size):
        return pl.ds(pl.multiple_of(index * size, size), size)

    def put(src, dst, phase, to):
        pltpu.make_async_remote_copy(
            src_ref=src, dst_ref=dst, send_sem=send.at[phase], recv_sem=recv.at[phase],
            device_id=to, device_id_type=MESH,
        ).start()

    def got(region, phase):
        pltpu.make_async_remote_copy(
            src_ref=region, dst_ref=region, send_sem=send.at[phase], recv_sem=recv.at[phase],
            device_id=partner, device_id_type=MESH,
        ).wait_recv()

    def sent(region, phase):
        pltpu.make_async_remote_copy(
            src_ref=region, dst_ref=region, send_sem=send.at[phase], recv_sem=recv.at[phase],
            device_id=partner, device_id_type=MESH,
        ).wait_send()

    def summed(ref, it, size, count):
        total = ref[it, 0:size, :].astype(F32)
        for k in range(1, count):
            total = total + ref[it, k * size : (k + 1) * size, :].astype(F32)
        return total

    greet = ring + [along_z(d, 1) for d in (4, -4, 3, -3, 2, -2, 1, -1)] + [partner]
    for o in FAR_XY:
        greet += [along_xy(*o), along_xy(*o, 1)]
    barrier = pltpu.get_barrier_semaphore()
    for to in greet:
        pl.semaphore_signal(barrier, inc=1, device_id=to, device_id_type=MESH)

    load_f = pltpu.make_async_copy(fac, f_v, load.at[8])
    load_f.start()
    loads = []
    for i in range(4):
        r = pl.ds(i * 128, 128)
        pair_in = [
            pltpu.make_async_copy(mom.at[0, r], m_v.at[r], load.at[2 * i]),
            pltpu.make_async_copy(grad.at[0, r], g_v.at[r], load.at[2 * i + 1]),
        ]
        for copy in pair_in:
            copy.start()
        loads.append(pair_in)
    load_f.wait()
    fb[...] = f_v[...].astype(BF16)
    for i in range(4):
        for copy in loads[i]:
            copy.wait()
        r = pl.ds(i * 128, 128)
        block = (m_v[r, :].astype(F32) + g_v[r, :].astype(F32)).astype(BF16)
        own[r, :] = block
        xs0[r, :] = (0.5 * jnp.dot(block, fb[...], preferred_element_type=F32)).astype(BF16)

    mine = pl.ds(pl.multiple_of(c * HALF, HALF), HALF)
    theirs = pl.ds(pl.multiple_of(other * HALF, HALF), HALF)
    nt = (((1,), (1,)), ((), ()))
    tn = (((0,), (0,)), ((), ()))

    def phase(it, k):
        return 2 + 8 * it + k

    def left_spread(it, total):
        xo[it] = total.astype(BF16)
        for to in ring:
            put(xo.at[it], xp.at[it, chunk(t, XCH)], phase(it, 1), to)
        xp[it, chunk(t, XCH), :] = total.astype(BF16)

    def left_here(it):
        got(xp.at[it, pl.ds(0, (NZ - 1) * XCH)], phase(it, 1))
        both = xp[it, 0:HALF, :].astype(F32) + xp[it, HALF : 2 * HALF, :].astype(F32)
        return both.astype(BF16)

    def right_out(it, left):
        part = lax.dot_general(left, own[mine, :], tn, preferred_element_type=F32)
        part = part + lax.dot_general(left, oth[...], tn, preferred_element_type=F32)
        part = (0.5 * part).astype(BF16)
        for i in range(TILES):
            ws[it, i * 128 : (i + 1) * 128, :] = part[:, i * 128 : (i + 1) * 128]
        for slot, to in near:
            there = to[0] * 8 + pair_of(to[1])

            @pl.when(there < PLACES)
            def _():
                put(ws.at[it, chunk(there, WCH)], wr.at[it, pl.ds(slot * WCH, WCH)], phase(it, 2), to)

        @pl.when(owner)
        def _():
            wr[it, 0:WCH, :] = ws[it, chunk(place, WCH), :]

    def right_spread(it):
        @pl.when(owner)
        def _():
            got(wr.at[it, pl.ds(WCH, 15 * WCH)], phase(it, 2))
            total = summed(wr, it, WCH, 16).astype(BF16)
            wo[it] = total
            rows = chunk(half * 8 + pair, WCH)
            for to in chips:
                put(wo.at[it], wp.at[it, rows], phase(it, 3), to)
            wp[it, rows, :] = total

    def right_join(it):
        @pl.when(c == 0)
        def _():
            got(wp.at[it, pl.ds(0, 15 * WCH)], phase(it, 3))
            both = wp[it, 0:512, :].astype(F32) + wp[it, 512:1024, :].astype(F32)
            wa[it, 0:512, :] = both.astype(BF16)
            put(wa.at[it, pl.ds(0, 512)], wa.at[it, pl.ds(0, 512)], phase(it, 4), partner)

        @pl.when(c == 1)
        def _():
            @pl.when(owner)
            def _():
                got(wp.at[it, pl.ds(0, 11 * WCH)], phase(it, 3))

            @pl.when(idle)
            def _():
                got(wp.at[it, pl.ds(0, 12 * WCH)], phase(it, 3))

            both = wp[it, 0:384, :].astype(F32) + wp[it, 512:896, :].astype(F32)
            wa[it, 512:896, :] = both.astype(BF16)
            put(wa.at[it, pl.ds(512, 384)], wa.at[it, pl.ds(512, 384)], phase(it, 4), partner)

    def right_here(it):
        @pl.when(c == 0)
        def _():
            got(wa.at[it, pl.ds(512, 384)], phase(it, 4))

        @pl.when(c == 1)
        def _():
            got(wa.at[it, pl.ds(0, 512)], phase(it, 4))

    def gram_out(it, left):
        gs[it] = lax.dot_general(left, left, tn, preferred_element_type=F32)
        for slot, to in near:
            there = to[0] * 8 + pair_of(to[1])
            put(gs.at[it, chunk(there, GCH)], gr.at[it, pl.ds(slot * GCH, GCH)], phase(it, 5), to)
        gr[it, 0:GCH, :] = gs[it, chunk(place, GCH), :]

    def gram_spread(it):
        got(gr.at[it, pl.ds(GCH, 15 * GCH)], phase(it, 5))
        total = summed(gr, it, GCH, 16)
        go[it] = total
        rows = chunk(half * 16 + place, GCH)
        for o in FAR_XY:
            for dc in (0, 1):
                put(go.at[it], gp.at[it, rows], phase(it, 6), along_xy(*o, dc))
        put(go.at[it], gp.at[it, rows], phase(it, 6), partner)
        gp[it, rows, :] = total

    def gram_here(it):
        got(gp.at[it, pl.ds(0, 31 * GCH)], phase(it, 6))
        return gp[it, 0:RANK, :] + gp[it, RANK : 2 * RANK, :]

    def squares_out(it, tiles):
        total = jnp.sum(tiles[0] * tiles[0], axis=0, keepdims=True)
        for tile in tiles[1:]:
            total = total + jnp.sum(tile * tile, axis=0, keepdims=True)
        qs[it] = jnp.broadcast_to(total, (8, RANK))
        for to in ring:
            put(qs.at[it], qr.at[it, chunk(t, 8)], phase(it, 7), to)
        qr[it, chunk(t, 8), :] = qs[it]

    def norms(it):
        got(qr.at[it, pl.ds(0, (NZ - 1) * 8)], phase(it, 7))
        return jnp.sqrt(summed(qr, it, 8, NZ)[0:1, :] + 1e-06)

    pl.semaphore_wait(barrier, len(greet))
    for d in NEAR_Z + [0]:
        for dc in (0, 1):
            if (d, dc) == (0, 0):
                continue
            to = along_z(d, dc)
            src = xs0.at[chunk(to[0] * 8 + lax.rem(to[2], 8), XCH)]
            put(src, xr0.at[0, pl.ds((2 * (d % 8) + dc) * XCH, XCH)], phase(0, 0), to)
    xr0[0, 0:XCH, :] = xs0[chunk(c * 8 + lax.rem(t, 8), XCH), :]
    put(own.at[theirs], oth, 0, partner)
    got(xr0.at[0, pl.ds(XCH, 15 * XCH)], phase(0, 0))
    left_spread(0, summed(xr0, 0, XCH, 16))
    got(oth, 0)
    left = left_here(0)
    right_out(0, left)
    gram_out(0, left)
    right_spread(0)
    gram_spread(0)
    right_join(0)

    def products(first, last):
        tiles = [wa[0, i * 128 : (i + 1) * 128, :] for i in range(first, last)]
        tiles = jnp.concatenate(tiles, 1)
        cols = pl.ds(first * 128, (last - first) * 128)
        part = lax.dot_general(own[mine, cols], tiles, nt, preferred_element_type=F32)
        return part + lax.dot_general(oth[:, cols], tiles, nt, preferred_element_type=F32)

    @pl.when(c == 0)
    def _():
        acc[...] = products(0, 4)

    @pl.when(c == 1)
    def _():
        acc[...] = products(4, 7)

    right_here(0)

    @pl.when(c == 0)
    def _():
        xs1[0] = (0.5 * (acc[...] + products(4, 7))).astype(BF16)

    @pl.when(c == 1)
    def _():
        xs1[0] = (0.5 * (acc[...] + products(0, 4))).astype(BF16)

    for d in NEAR_Z:
        to = along_z(d)
        src = xs1.at[0, chunk(lax.rem(to[2], 8), XCH)]
        put(src, xr1.at[0, pl.ds((d % 8) * XCH, XCH)], phase(1, 0), to)
    xr1[0, 0:XCH, :] = xs1[0, chunk(lax.rem(t, 8), XCH), :]
    a_s[...] = gram_here(0)
    inverse_cholesky(a_s, lower.at[0], range(8))
    got(xr1.at[0, pl.ds(XCH, 7 * XCH)], phase(1, 0))
    owned = summed(xr1, 0, XCH, 8)
    left_spread(
        1,
        lax.dot_general(owned, lower[0], nt, preferred_element_type=F32, precision=HIGHEST),
    )
    squares_out(0, right_times(wa.at[0], lower[0]))
    left = left_here(1)
    gram_out(1, left)
    right_out(1, left)
    xl[...] = left
    put(xl, xoth, 1, partner)
    gram_spread(1)
    right_spread(1)
    scale = jnp.broadcast_to(1.0 / norms(0), (RANK, RANK))
    a_s[...] = gram_here(1) * scale * scale.T
    inverse_cholesky(a_s, lower.at[1], range(4))
    right_join(1)
    inverse_cholesky(a_s, lower.at[1], range(4, 8))
    mix = lower[1] * scale
    right_here(1)
    tiles = right_times(wa.at[1], mix)
    squares_out(1, tiles)
    for i in range(TILES):
        right[i * 128 : (i + 1) * 128, :] = tiles[i]
    got(xoth, 1)
    ob[mine, :] = rows_times(xl[...], mix).astype(BF16)
    ob[theirs, :] = rows_times(xoth[...], mix).astype(BF16)
    right_b = right[...].astype(BF16)
    for i in range(4):
        r = pl.ds(i * 128, 128)
        feedback = lax.dot_general(ob[r, :], right_b, nt, preferred_element_type=F32)
        new_mom[0, r, :] = (own[r, :].astype(F32) - 0.05 * feedback).astype(BF16)

    sent(oth, 0)
    sent(xl, 1)
    sent(xr0.at[0, pl.ds(0, 15 * XCH)], phase(0, 0))
    sent(xr1.at[0, pl.ds(0, 7 * XCH)], phase(1, 0))
    for it in range(2):
        sent(xp.at[it, pl.ds(0, (NZ - 1) * XCH)], phase(it, 1))

        @pl.when(owner)
        def _():
            sent(wr.at[it, pl.ds(0, 13 * WCH)], phase(it, 2))
            sent(wr.at[it, pl.ds(0, 15 * WCH)], phase(it, 3))

        @pl.when(idle)
        def _():
            sent(wr.at[it, pl.ds(0, 14 * WCH)], phase(it, 2))

        @pl.when(c == 0)
        def _():
            sent(wa.at[it, pl.ds(0, 512)], phase(it, 4))

        @pl.when(c == 1)
        def _():
            sent(wa.at[it, pl.ds(512, 384)], phase(it, 4))

        sent(gr.at[it, pl.ds(0, 15 * GCH)], phase(it, 5))
        sent(gp.at[it, pl.ds(0, 31 * GCH)], phase(it, 6))
        sent(qr.at[it, pl.ds(0, (NZ - 1) * 8)], phase(it, 7))

    new_fac[...] = right[...] * (1.0 / norms(1))
    factor_b = new_fac[...].astype(BF16)
    for i in range(4):
        r = pl.ds(i * 128, 128)
        low_rank = lax.dot_general(ob[r, :], factor_b, nt, preferred_element_type=F32)
        update[r, :] = (math.sqrt(D * FF / RANK) * low_rank).astype(BF16)


def shards(momentum, gradient, right_factor):
    scratch = [
        pltpu.VMEM((ROWS, COLS), BF16),
        pltpu.VMEM((ROWS, COLS), BF16),
        pltpu.VMEM((COLS, RANK), F32),
        pltpu.VMEM((COLS, RANK), BF16),
        pltpu.VMEM((ROWS, COLS), BF16),
        pltpu.VMEM((HALF, COLS), BF16),
        pltpu.VMEM((ROWS, RANK), BF16),
        pltpu.VMEM((1, 16 * XCH, RANK), BF16),
        pltpu.VMEM((1, HALF, RANK), BF16),
        pltpu.VMEM((1, 8 * XCH, RANK), BF16),
        pltpu.VMEM((2, XCH, RANK), BF16),
        pltpu.VMEM((2, NZ * XCH, RANK), BF16),
        pltpu.VMEM((HALF, RANK), BF16),
        pltpu.VMEM((HALF, RANK), BF16),
        pltpu.VMEM((2, COLS, RANK), BF16),
        pltpu.VMEM((2, 16 * WCH, RANK), BF16),
        pltpu.VMEM((2, WCH, RANK), BF16),
        pltpu.VMEM((2, 16 * WCH, RANK), BF16),
        pltpu.VMEM((2, COLS, RANK), BF16),
        pltpu.VMEM((2, RANK, RANK), F32),
        pltpu.VMEM((2, 16 * GCH, RANK), F32),
        pltpu.VMEM((2, GCH, RANK), F32),
        pltpu.VMEM((2, 32 * GCH, RANK), F32),
        pltpu.VMEM((2, 8, RANK), F32),
        pltpu.VMEM((2, NZ * 8, RANK), F32),
        pltpu.VMEM((2, RANK, RANK), F32),
        pltpu.VMEM((RANK, RANK), F32),
        pltpu.VMEM((COLS, RANK), F32),
        pltpu.VMEM((ROWS, RANK), BF16),
        pltpu.VMEM((HALF, RANK), F32),
        pltpu.SemaphoreType.DMA((9,)),
        pltpu.SemaphoreType.DMA((18,)),
        pltpu.SemaphoreType.DMA((18,)),
    ]
    arguments = [
        pltpu.with_memory_space_constraint(v, pltpu.HBM)
        for v in (momentum, gradient, right_factor)
    ]
    return pl.pallas_call(
        kernel,
        out_shape=(
            jax.ShapeDtypeStruct((1, ROWS, COLS), BF16),
            jax.ShapeDtypeStruct((ROWS, COLS), BF16),
            jax.ShapeDtypeStruct((COLS, RANK), F32),
        ),
        in_specs=[pl.BlockSpec(memory_space=pl.ANY)] * 3,
        out_specs=(pl.BlockSpec(memory_space=pltpu.VMEM),) * 3,
        scratch_shapes=scratch,
        compiler_params=pltpu.CompilerParams(
            collective_id=0, has_side_effects=True, vmem_limit_bytes=40 * 2**20
        ),
        cost_estimate=pl.CostEstimate(
            flops=12 * ROWS * COLS * RANK, bytes_accessed=6 * 2**20, transcendentals=0
        ),
    )(*arguments)


def solution(mesh):
    placed = (P("dp", "fsdp", "tensor"), P("dp", "fsdp", "tensor"), P("tensor", None))
    return jax.shard_map(
        shards,
        mesh=mesh,
        in_specs=placed,
        out_specs=(P("dp", "fsdp", "tensor"), P("fsdp", "tensor"), P("tensor", None)),
        check_vma=False,
    )
```

time: 87.7 us -> 84.1 us (0.959)
  Pallas kernels: 82.5 us -> 80.7 us
  local copies, waits for them, and re-layouts: 4.35 us -> 2.61 us
    unnamed x7 -> x3, local copies, waits for them, and re-layouts: 4.35 us -> 2.61 us
    pallas_call x1, Pallas kernels: 82.5 us -> 80.7 us  [shards(): pl.pallas_call(kernel, out_shape=(jax.ShapeDtypeStruct((1, ROWS, COLS), B...]
where the time goes in v2:
time: 84.1 us; the launch traced here: 84 us
  Pallas kernels  80.7 us (96%)
  local copies, waits for them, and re-layouts  2.61 us (3%)
    pallas_call x1, Pallas kernels, shards(): pl.pallas_call(kernel, out_shape=(jax.ShapeDtypeStruct((1, ROWS, COLS), B...  80.7 us
    unnamed x3, local copies, waits for them, and re-layouts  2.61 us

profile of v2, /device:TPU:1, one launch (start us, length us, event | category | flops | bytes accessed | tf_op | source)
XLA Modules:
  0.0 84.0 jit_solution(3417851872900882417)
XLA Ops:
  0.6 80.7 %shard_map.58 = (bf16[1,512,896]{2,1,0:T(8,128)(2,1)S(1)}, bf16[512,896]{1,0:T(8,128)(2,1)S(1)}, f32[896,128]{1,0:T(8,128)S(1)}) custom-call(bf16[1,512,896]{2,1,0:T(8,128)(2,1)} %mom.1, bf16[1,512,896]{2,1,0:T(8,128)(2,1)} %grad.1, f32[896,128]{1,0:T(8,128)} %fac.1), custom_call_target="tpu_custom_call" | custom-call | flops 704643072 | bytes 6291456 | tf_op jit(solution)/shard_map/pallas_call | solution.py:479
  81.4 0.9 %copy.9 = bf16[1,512,896]{2,1,0:T(8,128)(2,1)} copy(bf16[1,512,896]{2,1,0:T(8,128)(2,1)S(1)} %get-tuple-element.6) | data formatting | bytes 1835008
  82.3 0.9 %copy.10 = bf16[512,896]{1,0:T(8,128)(2,1)} copy(bf16[512,896]{1,0:T(8,128)(2,1)S(1)} %get-tuple-element.7) | data formatting | bytes 1835008
  83.2 0.8 copy.11

commit v3 on v2

--- a/solution.py
+++ b/solution.py
@@ -13,7 +13,6 @@
 MESH = pl.DeviceIdType.MESH
 F32 = jnp.float32
 BF16 = jnp.bfloat16
-HIGHEST = lax.Precision.HIGHEST
 
 NZ = 16
 ROWS = 512
@@ -93,26 +92,25 @@
 
 
 def right_times(tiles_ref, m):
-    parts = jnp.concatenate(split3(m), 0)
+    parts = jnp.concatenate(split3(m)[:2], 0)
     out = []
     for i in range(TILES):
         tile = tiles_ref[i * 128 : (i + 1) * 128, :]
         r = lax.dot_general(tile, parts, (((0,), (1,)), ((), ())), preferred_element_type=F32)
-        out.append(r[:, :RANK] + (r[:, RANK : 2 * RANK] + r[:, 2 * RANK :]))
+        out.append(r[:, :RANK] + r[:, RANK:])
     return out
 
 
 def rows_times(x, m):
-    r = lax.dot_general(
-        x, jnp.concatenate(split3(m), 0), (((1,), (1,)), ((), ())), preferred_element_type=F32
-    )
-    return r[:, :RANK] + (r[:, RANK : 2 * RANK] + r[:, 2 * RANK :])
+    parts = jnp.concatenate(split3(m)[:2], 0)
+    r = lax.dot_general(x, parts, (((1,), (1,)), ((), ())), preferred_element_type=F32)
+    return r[:, :RANK] + r[:, RANK:]
 
 
 def kernel(
-    mom, grad, fac, new_mom, update, new_fac,
-    m_v, g_v, f_v, fb, own, oth, xs0, xr0, xs1, xr1, xo, xp, xl, xoth, ws, wr, wo, wp, wa, gs, gr, go, gp,
-    qs, qr, lower, a_s, right, ob, acc, load, send, recv,
+    mom, grad, fac, new_mom, right, ob, norm,
+    m_v, g_v, f_v, fb, own, oth, xs0, xr0, xs1, xr1, xo, xp, xl, xoth, ws, wr, wo, wp, wa, gs, gr, go, gp, ga,
+    qs, qr, lower, a_s, acc, load, send, recv,
 ):
     c = lax.axis_index("dp")
     f = lax.axis_index("fsdp")
@@ -172,7 +170,7 @@
             total = total + ref[it, k * size : (k + 1) * size, :].astype(F32)
         return total
 
-    greet = ring + [along_z(d, 1) for d in (4, -4, 3, -3, 2, -2, 1, -1)] + [partner]
+    greet = [along_z(d, dc) for d in (4, -4, 3, -3, 2, -2, 1, -1) for dc in (0, 1)] + [partner]
     for o in FAR_XY:
         greet += [along_xy(*o), along_xy(*o, 1)]
     barrier = pltpu.get_barrier_semaphore()
@@ -207,7 +205,7 @@
     tn = (((0,), (0,)), ((), ()))
 
     def phase(it, k):
-        return 2 + 8 * it + k
+        return 2 + 9 * it + k
 
     def left_spread(it, total):
         xo[it] = total.astype(BF16)
@@ -290,16 +288,20 @@
         got(gr.at[it, pl.ds(GCH, 15 * GCH)], phase(it, 5))
         total = summed(gr, it, GCH, 16)
         go[it] = total
-        rows = chunk(half * 16 + place, GCH)
-        for o in FAR_XY:
-            for dc in (0, 1):
-                put(go.at[it], gp.at[it, rows], phase(it, 6), along_xy(*o, dc))
-        put(go.at[it], gp.at[it, rows], phase(it, 6), partner)
+        rows = chunk(half * 8 + pair, GCH)
+        for to in chips:
+            put(go.at[it], gp.at[it, rows], phase(it, 6), to)
         gp[it, rows, :] = total
 
+    def gram_join(it):
+        got(gp.at[it, pl.ds(0, 15 * GCH)], phase(it, 6))
+        rows = chunk(c, RANK // 2)
+        ga[it, rows, :] = gp[it, 0 : RANK // 2, :] + gp[it, RANK // 2 : RANK, :]
+        put(ga.at[it, rows], ga.at[it, rows], phase(it, 8), partner)
+
     def gram_here(it):
-        got(gp.at[it, pl.ds(0, 31 * GCH)], phase(it, 6))
-        return gp[it, 0:RANK, :] + gp[it, RANK : 2 * RANK, :]
+        got(ga.at[it, pl.ds(0, RANK // 2)], phase(it, 8))
+        return ga[it]
 
     def squares_out(it, tiles):
         total = jnp.sum(tiles[0] * tiles[0], axis=0, keepdims=True)
@@ -364,14 +366,15 @@
         src = xs1.at[0, chunk(lax.rem(to[2], 8), XCH)]
         put(src, xr1.at[0, pl.ds((d % 8) * XCH, XCH)], phase(1, 0), to)
     xr1[0, 0:XCH, :] = xs1[0, chunk(lax.rem(t, 8), XCH), :]
+    gram_join(0)
     a_s[...] = gram_here(0)
     inverse_cholesky(a_s, lower.at[0], range(8))
+    low_parts = split3(lower[0])
+    low_parts = jnp.concatenate([low_parts[0], low_parts[1], low_parts[0]], 1)
     got(xr1.at[0, pl.ds(XCH, 7 * XCH)], phase(1, 0))
-    owned = summed(xr1, 0, XCH, 8)
-    left_spread(
-        1,
-        lax.dot_general(owned, lower[0], nt, preferred_element_type=F32, precision=HIGHEST),
-    )
+    owned = split3(summed(xr1, 0, XCH, 8))
+    owned = jnp.concatenate([owned[0], owned[0], owned[1]], 1)
+    left_spread(1, lax.dot_general(owned, low_parts, nt, preferred_element_type=F32))
     squares_out(0, right_times(wa.at[0], lower[0]))
     left = left_here(1)
     gram_out(1, left)
@@ -381,6 +384,7 @@
     gram_spread(1)
     right_spread(1)
     scale = jnp.broadcast_to(1.0 / norms(0), (RANK, RANK))
+    gram_join(1)
     a_s[...] = gram_here(1) * scale * scale.T
     inverse_cholesky(a_s, lower.at[1], range(4))
     right_join(1)
@@ -425,15 +429,30 @@
             sent(wa.at[it, pl.ds(512, 384)], phase(it, 4))
 
         sent(gr.at[it, pl.ds(0, 15 * GCH)], phase(it, 5))
-        sent(gp.at[it, pl.ds(0, 31 * GCH)], phase(it, 6))
+        sent(gp.at[it, pl.ds(0, 15 * GCH)], phase(it, 6))
+        sent(ga.at[it, pl.ds(0, RANK // 2)], phase(it, 8))
         sent(qr.at[it, pl.ds(0, (NZ - 1) * 8)], phase(it, 7))
 
-    new_fac[...] = right[...] * (1.0 / norms(1))
-    factor_b = new_fac[...].astype(BF16)
+    norm[...] = jnp.broadcast_to(1.0 / norms(1), (8, RANK))
+
+
+def finish(new_mom, right, ob, norm, new_mom_out, update, new_fac, fac, up, sem):
+    first = pltpu.make_async_copy(new_mom, new_mom_out, sem.at[0])
+    first.start()
+    fac[...] = right[...] * norm[0:1, :]
+    copies = [first, pltpu.make_async_copy(fac, new_fac, sem.at[1])]
+    copies[1].start()
+    factor_b = fac[...].astype(BF16)
+    nt = (((1,), (1,)), ((), ()))
     for i in range(4):
         r = pl.ds(i * 128, 128)
         low_rank = lax.dot_general(ob[r, :], factor_b, nt, preferred_element_type=F32)
-        update[r, :] = (math.sqrt(D * FF / RANK) * low_rank).astype(BF16)
+        up[r, :] = (math.sqrt(D * FF / RANK) * low_rank).astype(BF16)
+        copy = pltpu.make_async_copy(up.at[r], update.at[r], sem.at[2 + i])
+        copy.start()
+        copies.append(copy)
+    for copy in copies:
+        copy.wait()
 
 
 def shards(momentum, gradient, right_factor):
@@ -460,39 +479,60 @@
         pltpu.VMEM((2, RANK, RANK), F32),
         pltpu.VMEM((2, 16 * GCH, RANK), F32),
         pltpu.VMEM((2, GCH, RANK), F32),
-        pltpu.VMEM((2, 32 * GCH, RANK), F32),
+        pltpu.VMEM((2, 16 * GCH, RANK), F32),
+        pltpu.VMEM((2, RANK, RANK), F32),
         pltpu.VMEM((2, 8, RANK), F32),
         pltpu.VMEM((2, NZ * 8, RANK), F32),
         pltpu.VMEM((2, RANK, RANK), F32),
         pltpu.VMEM((RANK, RANK), F32),
-        pltpu.VMEM((COLS, RANK), F32),
-        pltpu.VMEM((ROWS, RANK), BF16),
         pltpu.VMEM((HALF, RANK), F32),
         pltpu.SemaphoreType.DMA((9,)),
-        pltpu.SemaphoreType.DMA((18,)),
-        pltpu.SemaphoreType.DMA((18,)),
+        pltpu.SemaphoreType.DMA((20,)),
+        pltpu.SemaphoreType.DMA((20,)),
     ]
     arguments = [
         pltpu.with_memory_space_constraint(v, pltpu.HBM)
         for v in (momentum, gradient, right_factor)
     ]
+    vmem = pl.BlockSpec(memory_space=pltpu.VMEM)
+    anywhere = pl.BlockSpec(memory_space=pl.ANY)
+    made = pl.pallas_call(
+        kernel,
+        out_shape=(
+            jax.ShapeDtypeStruct((1, ROWS, COLS), BF16),
+            jax.ShapeDtypeStruct((COLS, RANK), F32),
+            jax.ShapeDtypeStruct((ROWS, RANK), BF16),
+            jax.ShapeDtypeStruct((8, RANK), F32),
+        ),
+        in_specs=[anywhere] * 3,
+        out_specs=(vmem,) * 4,
+        scratch_shapes=scratch,
+        compiler_params=pltpu.CompilerParams(
+            collective_id=0, has_side_effects=True, vmem_limit_bytes=40 * 2**20
+        ),
+        cost_estimate=pl.CostEstimate(
+            flops=10 * ROWS * COLS * RANK, bytes_accessed=4 * 2**20, transcendentals=0
+        ),
+    )(*arguments)
     return pl.pallas_call(
-        kernel,
+        finish,
         out_shape=(
             jax.ShapeDtypeStruct((1, ROWS, COLS), BF16),
             jax.ShapeDtypeStruct((ROWS, COLS), BF16),
             jax.ShapeDtypeStruct((COLS, RANK), F32),
         ),
-        in_specs=[pl.BlockSpec(memory_space=pl.ANY)] * 3,
-        out_specs=(pl.BlockSpec(memory_space=pltpu.VMEM),) * 3,
-        scratch_shapes=scratch,
-        compiler_params=pltpu.CompilerParams(
-            collective_id=0, has_side_effects=True, vmem_limit_bytes=40 * 2**20
+        in_specs=[vmem] * 4,
+        out_specs=(anywhere,) * 3,
+        scratch_shapes=[
+            pltpu.VMEM((COLS, RANK), F32),
+            pltpu.VMEM((ROWS, COLS), BF16),
+            pltpu.SemaphoreType.DMA((6,)),
+        ],
+        compiler_params=pltpu.CompilerParams(vmem_limit_bytes=40 * 2**20),
+        cost_estimate=pl.CostEstimate(
+            flops=2 * ROWS * COLS * RANK, bytes_accessed=3 * 2**20, transcendentals=0
         ),
-        cost_estimate=pl.CostEstimate(
-            flops=12 * ROWS * COLS * RANK, bytes_accessed=6 * 2**20, transcendentals=0
-        ),
-    )(*arguments)
+    )(*made)
 
 
 def solution(mesh):

time: 84.1 us -> 80.1 us (0.952)
  local copies, waits for them, and re-layouts: 2.61 us -> 0 us
  Pallas kernels: 80.7 us -> 79.3 us
    pallas_call x1, Pallas kernels: 80.7 us -> 77.9 us  [shards(): pl.pallas_call(kernel, out_shape=(jax.ShapeDtypeStruct((1, ROWS, COLS), B...]
    unnamed x3 -> x0, local copies, waits for them, and re-layouts: 2.61 us -> none
    pallas_call x0 -> x1, Pallas kernels: none -> 1.42 us  [shards(): pl.pallas_call(finish, out_shape=(jax.ShapeDtypeStruct((1, ROWS, COLS), B...]
where the time goes in v3:
time: 80.1 us; the launch traced here: 79.9 us
  Pallas kernels  79.3 us (99%)
    pallas_call x1, Pallas kernels, shards(): pl.pallas_call(kernel, out_shape=(jax.ShapeDtypeStruct((1, ROWS, COLS), B...  77.9 us

profile of v3, /device:TPU:1, one launch (start us, length us, event | category | flops | bytes accessed | tf_op | source)
XLA Modules:
  0.0 79.9 jit_solution(16295292225358453342)
XLA Ops:
  0.6 77.9 %shard_map.58 = (bf16[1,512,896]{2,1,0:T(8,128)(2,1)S(1)}, f32[896,128]{1,0:T(8,128)S(1)}, bf16[512,128]{1,0:T(8,128)(2,1)S(1)}, f32[8,128]{1,0:T(8,128)S(1)}) custom-call(bf16[1,512,896]{2,1,0:T(8,128)(2,1)} %mom.1, bf16[1,512,896]{2,1,0:T(8,128)(2,1)} %grad.1, f32[896,128]{1,0:T(8,128)} %fac.1), custom_call_target="tpu_custom_call" | custom-call | flops 587202560 | bytes 4194304 | tf_op jit(solution)/shard_map/pallas_call | solution.py:499
  78.5 1.4 %shard_map.59 = (bf16[1,512,896]{2,1,0:T(8,128)(2,1)}, bf16[512,896]{1,0:T(8,128)(2,1)}, f32[896,128]{1,0:T(8,128)}) custom-call(bf16[1,512,896]{2,1,0:T(8,128)(2,1)S(1)} %get-tuple-element.7.new_mom, f32[896,128]{1,0:T(8,128)S(1)} %get-tuple-element.8.right, bf16[512,128]{1,0:T(8,128)(2,1)S(1)} %get-tuple-element.9.ob, f32[8,128]{1,0:T(8,128)S(1)} %get-tuple-element.10.norm), custom_call_target="tpu_custom_call" | custom-call | flops 117440512 | bytes 3145728 | tf_op jit(solution)/shard_map/pallas_call | solution.py:517

commit v4 on v3

--- a/solution.py
+++ b/solution.py
@@ -109,7 +109,7 @@
 
 def kernel(
     mom, grad, fac, new_mom, right, ob, norm,
-    m_v, g_v, f_v, fb, own, oth, xs0, xr0, xs1, xr1, xo, xp, xl, xoth, ws, wr, wo, wp, wa, gs, gr, go, gp, ga,
+    m_v, g_v, f_v, fb, own, oth, xs0, xr0, xs1, xr1, xo, xp, xl, xoth, ws, wr, wo, wp, wa, gs, gr, go, gp0, gp1, ga,
     qs, qr, lower, a_s, acc, load, send, recv,
 ):
     c = lax.axis_index("dp")
@@ -170,13 +170,17 @@
             total = total + ref[it, k * size : (k + 1) * size, :].astype(F32)
         return total
 
-    greet = [along_z(d, dc) for d in (4, -4, 3, -3, 2, -2, 1, -1) for dc in (0, 1)] + [partner]
-    for o in FAR_XY:
-        greet += [along_xy(*o), along_xy(*o, 1)]
+    greet = [along_z(d, dc) for d in (4, -4) for dc in (0, 1)]
+    greet += [along_xy(*o, dc) for o in FAR_XY[:5] for dc in (0, 1)]
+    greet += [along_z(d, dc) for d in (3, -3, 2, -2, 1, -1) for dc in (0, 1)]
+    greet += [along_xy(*o, dc) for o in FAR_XY[5:] for dc in (0, 1)] + [partner]
     barrier = pltpu.get_barrier_semaphore()
-    for to in greet:
-        pl.semaphore_signal(barrier, inc=1, device_id=to, device_id_type=MESH)
-
+
+    def signal(some):
+        for to in some:
+            pl.semaphore_signal(barrier, inc=1, device_id=to, device_id_type=MESH)
+
+    signal(greet[:14])
     load_f = pltpu.make_async_copy(fac, f_v, load.at[8])
     load_f.start()
     loads = []
@@ -189,6 +193,7 @@
         for copy in pair_in:
             copy.start()
         loads.append(pair_in)
+    signal(greet[14:])
     load_f.wait()
     fb[...] = f_v[...].astype(BF16)
     for i in range(4):
@@ -284,30 +289,45 @@
             put(gs.at[it, chunk(there, GCH)], gr.at[it, pl.ds(slot * GCH, GCH)], phase(it, 5), to)
         gr[it, 0:GCH, :] = gs[it, chunk(place, GCH), :]
 
-    def gram_spread(it):
+    def gram_owned(it):
         got(gr.at[it, pl.ds(GCH, 15 * GCH)], phase(it, 5))
         total = summed(gr, it, GCH, 16)
         go[it] = total
+        return total
+
+    def gram_spread_core(total):
         rows = chunk(half * 8 + pair, GCH)
         for to in chips:
-            put(go.at[it], gp.at[it, rows], phase(it, 6), to)
-        gp[it, rows, :] = total
-
-    def gram_join(it):
-        got(gp.at[it, pl.ds(0, 15 * GCH)], phase(it, 6))
+            put(go.at[0], gp0.at[0, rows], phase(0, 6), to)
+        gp0[0, rows, :] = total
+
+    def gram_join_core():
+        got(gp0.at[0, pl.ds(0, 15 * GCH)], phase(0, 6))
         rows = chunk(c, RANK // 2)
-        ga[it, rows, :] = gp[it, 0 : RANK // 2, :] + gp[it, RANK // 2 : RANK, :]
-        put(ga.at[it, rows], ga.at[it, rows], phase(it, 8), partner)
-
-    def gram_here(it):
-        got(ga.at[it, pl.ds(0, RANK // 2)], phase(it, 8))
-        return ga[it]
-
-    def squares_out(it, tiles):
+        ga[rows, :] = gp0[0, 0 : RANK // 2, :] + gp0[0, RANK // 2 : RANK, :]
+        put(ga.at[rows], ga.at[rows], phase(0, 8), partner)
+        got(ga.at[pl.ds(0, RANK // 2)], phase(0, 8))
+        return ga[...]
+
+    def gram_spread_all(total):
+        rows = chunk(half * 16 + place, GCH)
+        for o in FAR_XY:
+            for dc in (0, 1):
+                put(go.at[1], gp1.at[0, rows], phase(1, 6), along_xy(*o, dc))
+        put(go.at[1], gp1.at[0, rows], phase(1, 6), partner)
+        gp1[0, rows, :] = total
+
+    def gram_join_all():
+        got(gp1.at[0, pl.ds(0, 31 * GCH)], phase(1, 6))
+        return gp1[0, 0:RANK, :] + gp1[0, RANK : 2 * RANK, :]
+
+    def squares_sum(it, tiles):
         total = jnp.sum(tiles[0] * tiles[0], axis=0, keepdims=True)
         for tile in tiles[1:]:
             total = total + jnp.sum(tile * tile, axis=0, keepdims=True)
         qs[it] = jnp.broadcast_to(total, (8, RANK))
+
+    def squares_send(it):
         for to in ring:
             put(qs.at[it], qr.at[it, chunk(t, 8)], phase(it, 7), to)
         qr[it, chunk(t, 8), :] = qs[it]
@@ -333,7 +353,7 @@
     right_out(0, left)
     gram_out(0, left)
     right_spread(0)
-    gram_spread(0)
+    gram_spread_core(gram_owned(0))
     right_join(0)
 
     def products(first, last):
@@ -366,8 +386,7 @@
         src = xs1.at[0, chunk(lax.rem(to[2], 8), XCH)]
         put(src, xr1.at[0, pl.ds((d % 8) * XCH, XCH)], phase(1, 0), to)
     xr1[0, 0:XCH, :] = xs1[0, chunk(lax.rem(t, 8), XCH), :]
-    gram_join(0)
-    a_s[...] = gram_here(0)
+    a_s[...] = gram_join_core()
     inverse_cholesky(a_s, lower.at[0], range(8))
     low_parts = split3(lower[0])
     low_parts = jnp.concatenate([low_parts[0], low_parts[1], low_parts[0]], 1)
@@ -375,24 +394,25 @@
     owned = split3(summed(xr1, 0, XCH, 8))
     owned = jnp.concatenate([owned[0], owned[0], owned[1]], 1)
     left_spread(1, lax.dot_general(owned, low_parts, nt, preferred_element_type=F32))
-    squares_out(0, right_times(wa.at[0], lower[0]))
+    squares_sum(0, right_times(wa.at[0], lower[0]))
     left = left_here(1)
     gram_out(1, left)
     right_out(1, left)
     xl[...] = left
     put(xl, xoth, 1, partner)
-    gram_spread(1)
+    squares_send(0)
+    gram_spread_all(gram_owned(1))
     right_spread(1)
     scale = jnp.broadcast_to(1.0 / norms(0), (RANK, RANK))
-    gram_join(1)
-    a_s[...] = gram_here(1) * scale * scale.T
+    a_s[...] = gram_join_all() * scale * scale.T
     inverse_cholesky(a_s, lower.at[1], range(4))
     right_join(1)
     inverse_cholesky(a_s, lower.at[1], range(4, 8))
     mix = lower[1] * scale
     right_here(1)
     tiles = right_times(wa.at[1], mix)
-    squares_out(1, tiles)
+    squares_sum(1, tiles)
+    squares_send(1)
     for i in range(TILES):
         right[i * 128 : (i + 1) * 128, :] = tiles[i]
     got(xoth, 1)
@@ -408,6 +428,9 @@
     sent(xl, 1)
     sent(xr0.at[0, pl.ds(0, 15 * XCH)], phase(0, 0))
     sent(xr1.at[0, pl.ds(0, 7 * XCH)], phase(1, 0))
+    sent(gp0.at[0, pl.ds(0, 15 * GCH)], phase(0, 6))
+    sent(ga.at[pl.ds(0, RANK // 2)], phase(0, 8))
+    sent(gp1.at[0, pl.ds(0, 31 * GCH)], phase(1, 6))
     for it in range(2):
         sent(xp.at[it, pl.ds(0, (NZ - 1) * XCH)], phase(it, 1))
 
@@ -429,8 +452,6 @@
             sent(wa.at[it, pl.ds(512, 384)], phase(it, 4))
 
         sent(gr.at[it, pl.ds(0, 15 * GCH)], phase(it, 5))
-        sent(gp.at[it, pl.ds(0, 15 * GCH)], phase(it, 6))
-        sent(ga.at[it, pl.ds(0, RANK // 2)], phase(it, 8))
         sent(qr.at[it, pl.ds(0, (NZ - 1) * 8)], phase(it, 7))
 
     norm[...] = jnp.broadcast_to(1.0 / norms(1), (8, RANK))
@@ -479,8 +500,9 @@
         pltpu.VMEM((2, RANK, RANK), F32),
         pltpu.VMEM((2, 16 * GCH, RANK), F32),
         pltpu.VMEM((2, GCH, RANK), F32),
-        pltpu.VMEM((2, 16 * GCH, RANK), F32),
-        pltpu.VMEM((2, RANK, RANK), F32),
+        pltpu.VMEM((1, 16 * GCH, RANK), F32),
+        pltpu.VMEM((1, 32 * GCH, RANK), F32),
+        pltpu.VMEM((RANK, RANK), F32),
         pltpu.VMEM((2, 8, RANK), F32),
         pltpu.VMEM((2, NZ * 8, RANK), F32),
         pltpu.VMEM((2, RANK, RANK), F32),

time: 80.1 us -> 78.9 us (0.985)
  Pallas kernels: 79.3 us -> 78 us
    pallas_call x1, Pallas kernels: 77.9 us -> 76.5 us  [shards(): pl.pallas_call(kernel, out_shape=(jax.ShapeDtypeStruct((1, ROWS, COLS), B...]
where the time goes in v4:
time: 78.9 us; the launch traced here: 78.6 us
  Pallas kernels  78 us (99%)
    pallas_call x1, Pallas kernels, shards(): pl.pallas_call(kernel, out_shape=(jax.ShapeDtypeStruct((1, ROWS, COLS), B...  76.5 us

profile of v4, /device:TPU:1, one launch (start us, length us, event | category | flops | bytes accessed | tf_op | source)
XLA Modules:
  0.0 78.6 jit_solution(2513655069592021383)
XLA Ops:
  0.6 76.5 %shard_map.58 = (bf16[1,512,896]{2,1,0:T(8,128)(2,1)S(1)}, f32[896,128]{1,0:T(8,128)S(1)}, bf16[512,128]{1,0:T(8,128)(2,1)S(1)}, f32[8,128]{1,0:T(8,128)S(1)}) custom-call(bf16[1,512,896]{2,1,0:T(8,128)(2,1)} %mom.1, bf16[1,512,896]{2,1,0:T(8,128)(2,1)} %grad.1, f32[896,128]{1,0:T(8,128)} %fac.1), custom_call_target="tpu_custom_call" | custom-call | flops 587202560 | bytes 4194304 | tf_op jit(solution)/shard_map/pallas_call | solution.py:521
  77.2 1.4 %shard_map.59 = (bf16[1,512,896]{2,1,0:T(8,128)(2,1)}, bf16[512,896]{1,0:T(8,128)(2,1)}, f32[896,128]{1,0:T(8,128)}) custom-call(bf16[1,512,896]{2,1,0:T(8,128)(2,1)S(1)} %get-tuple-element.7.new_mom, f32[896,128]{1,0:T(8,128)S(1)} %get-tuple-element.8.right, bf16[512,128]{1,0:T(8,128)(2,1)S(1)} %get-tuple-element.9.ob, f32[8,128]{1,0:T(8,128)S(1)} %get-tuple-element.10.norm), custom_call_target="tpu_custom_call" | custom-call | flops 117440512 | bytes 3145728 | tf_op jit(solution)/shard_map/pallas_call | solution.py:539

commit v5 on v4

--- a/solution.py
+++ b/solution.py
@@ -42,14 +42,6 @@
     return high, mid, low
 
 
-def outer_f32(u, v):
-    u1, u2, u3 = split3(u)
-    v1, v2, v3 = split3(v)
-    left = jnp.concatenate([u1, u1, u2, u1, u2, u3], 0)
-    right = jnp.concatenate([v1, v2, v1, v3, v2, v1], 0)
-    return lax.dot_general(left, right, (((0,), (0,)), ((), ())), preferred_element_type=F32)
-
-
 def inverse_cholesky(a_ref, e_ref, panels):
     if panels[0] == 0:
         rows = lax.broadcasted_iota(jnp.int32, (RANK, RANK), 0)
@@ -61,40 +53,40 @@
         return jnp.broadcast_to(t[j : j + 1, :], (NB, RANK))
 
     for base in [p * NB for p in panels]:
-        xa = a_ref[base : base + NB, :]
-        xe = e_ref[base : base + NB, :]
+        last = base + NB
+        xa = a_ref[base:last, :]
+        xe = e_ref[base:last, :]
         col = [
             jnp.broadcast_to(xa[:, base + k : base + k + 1], (NB, RANK)) for k in range(NB)
         ]
-        va, ve, out = [], [], []
+        if last < RANK:
+            c1, c2, c3 = split3(a_ref[last:, base:last])
+            below = jnp.concatenate([c1, c1, c2, c1, c2, c3], 1)
+        inverses = jnp.zeros((NB, RANK), F32)
+        out = jnp.zeros((NB, RANK), F32)
         for j in range(NB):
-            pivot = spread(col[j], j)
-            inv = 1.0 / pivot
+            inv = 1.0 / spread(col[j], j)
+            inverses = jnp.where(sub == j, inv, inverses)
             row_e = spread(xe, j)
-            out.append((row_e * lax.rsqrt(pivot))[0:1])
-            row_a = inv * spread(xa, j)
-            row_e = inv * row_e
-            va.append(row_a[0:1])
-            ve.append(row_e[0:1])
-            if j + 1 < NB:
-                below = jnp.where(sub > j, col[j], 0.0)
-                xa = xa - below * row_a
-                xe = xe - below * row_e
-                for k in range(j + 1, NB):
-                    col[k] = col[k] - below * (inv * spread(col[k], j))
-        last = base + NB
+            out = jnp.where(sub == j, row_e, out)
+            factor = jnp.where(sub != j, col[j] * inv, 0.0)
+            xa = xa - factor * spread(xa, j)
+            xe = xe - factor * row_e
+            for k in range(j + 1, NB):
+                col[k] = col[k] - factor * spread(col[k], j)
+        e_ref[base:last, :] = out * jnp.sqrt(inverses)
         if last < RANK:
-            v = jnp.concatenate([jnp.concatenate(va, 0), jnp.concatenate(ve, 0)], 1)
-            change = outer_f32(xa, v)
-            a_ref[last:, :] = a_ref[last:, :] - change[last:, :RANK]
-            e_ref[last:, :] = e_ref[last:, :] - change[last:, RANK:]
-        e_ref[base:last, :] = jnp.concatenate(out, 0)
-
-
-def right_times(tiles_ref, m):
+            v1, v2, v3 = split3(jnp.concatenate([xa * inverses, xe * inverses], 1))
+            solved = jnp.concatenate([v1, v2, v1, v3, v2, v1], 0)
+            change = jnp.dot(below, solved, preferred_element_type=F32)
+            a_ref[last:, :] = a_ref[last:, :] - change[:, :RANK]
+            e_ref[last:, :] = e_ref[last:, :] - change[:, RANK:]
+
+
+def right_times(tiles_ref, m, first=0, last=TILES):
     parts = jnp.concatenate(split3(m)[:2], 0)
     out = []
-    for i in range(TILES):
+    for i in range(first, last):
         tile = tiles_ref[i * 128 : (i + 1) * 128, :]
         r = lax.dot_general(tile, parts, (((0,), (1,)), ((), ())), preferred_element_type=F32)
         out.append(r[:, :RANK] + r[:, RANK:])
@@ -110,7 +102,7 @@
 def kernel(
     mom, grad, fac, new_mom, right, ob, norm,
     m_v, g_v, f_v, fb, own, oth, xs0, xr0, xs1, xr1, xo, xp, xl, xoth, ws, wr, wo, wp, wa, gs, gr, go, gp0, gp1, ga,
-    qs, qr, lower, a_s, acc, load, send, recv,
+    qs, qr0, qr1, lower, a_s, acc, tally, load, send, recv,
 ):
     c = lax.axis_index("dp")
     f = lax.axis_index("fsdp")
@@ -125,6 +117,9 @@
 
     def along_z(d, dc=0):
         return (core(dc), f, lax.rem(t + d + NZ, NZ))
+
+    def near_z(d, dc=0):
+        return along_z(4 + 8 * lax.rem(t, 2) if d == 4 else d, dc)
 
     def along_xy(dx, dy, dc=0):
         return (core(dc), lax.rem(x + dx, 4) * 4 + lax.rem(y + dy, 4), t)
@@ -148,19 +143,20 @@
 
     def put(src, dst, phase, to):
         pltpu.make_async_remote_copy(
-            src_ref=src, dst_ref=dst, send_sem=send.at[phase], recv_sem=recv.at[phase],
+            src_ref=src, dst_ref=dst, send_sem=send, recv_sem=recv.at[phase],
             device_id=to, device_id_type=MESH,
         ).start()
 
     def got(region, phase):
         pltpu.make_async_remote_copy(
-            src_ref=region, dst_ref=region, send_sem=send.at[phase], recv_sem=recv.at[phase],
+            src_ref=region, dst_ref=region, send_sem=send, recv_sem=recv.at[phase],
             device_id=partner, device_id_type=MESH,
         ).wait_recv()
 
-    def sent(region, phase):
+    def all_sent(rows):
+        region = tally.at[pl.ds(0, rows)]
         pltpu.make_async_remote_copy(
-            src_ref=region, dst_ref=region, send_sem=send.at[phase], recv_sem=recv.at[phase],
+            src_ref=region, dst_ref=region, send_sem=send, recv_sem=recv.at[0],
             device_id=partner, device_id_type=MESH,
         ).wait_send()
 
@@ -181,24 +177,22 @@
             pl.semaphore_signal(barrier, inc=1, device_id=to, device_id_type=MESH)
 
     signal(greet[:14])
-    load_f = pltpu.make_async_copy(fac, f_v, load.at[8])
+    load_f = pltpu.make_async_copy(fac, f_v, load.at[4])
     load_f.start()
-    loads = []
     for i in range(4):
         r = pl.ds(i * 128, 128)
         pair_in = [
-            pltpu.make_async_copy(mom.at[0, r], m_v.at[r], load.at[2 * i]),
-            pltpu.make_async_copy(grad.at[0, r], g_v.at[r], load.at[2 * i + 1]),
+            pltpu.make_async_copy(mom.at[0, r], m_v.at[r], load.at[i]),
+            pltpu.make_async_copy(grad.at[0, r], g_v.at[r], load.at[i]),
         ]
         for copy in pair_in:
             copy.start()
-        loads.append(pair_in)
     signal(greet[14:])
     load_f.wait()
     fb[...] = f_v[...].astype(BF16)
     for i in range(4):
-        for copy in loads[i]:
-            copy.wait()
+        both = tally.at[pl.ds(0, 2 * 128 * TILES)]
+        pltpu.make_async_copy(both, both, load.at[i]).wait()
         r = pl.ds(i * 128, 128)
         block = (m_v[r, :].astype(F32) + g_v[r, :].astype(F32)).astype(BF16)
         own[r, :] = block
@@ -325,23 +319,35 @@
         total = jnp.sum(tiles[0] * tiles[0], axis=0, keepdims=True)
         for tile in tiles[1:]:
             total = total + jnp.sum(tile * tile, axis=0, keepdims=True)
-        qs[it] = jnp.broadcast_to(total, (8, RANK))
-
-    def squares_send(it):
+        qs[it] = total
+
+    def squares_send_core():
         for to in ring:
-            put(qs.at[it], qr.at[it, chunk(t, 8)], phase(it, 7), to)
-        qr[it, chunk(t, 8), :] = qs[it]
+            put(qs.at[0], qr0.at[t], phase(0, 7), to)
+        qr0[t] = qs[0]
+
+    def squares_send_all():
+        slot = 2 * t + c
+        for d in FAR_Z:
+            for dc in (0, 1):
+                put(qs.at[1], qr1.at[slot], phase(1, 7), along_z(d, dc))
+        put(qs.at[1], qr1.at[slot], phase(1, 7), partner)
+        qr1[slot] = qs[1]
 
     def norms(it):
-        got(qr.at[it, pl.ds(0, (NZ - 1) * 8)], phase(it, 7))
-        return jnp.sqrt(summed(qr, it, 8, NZ)[0:1, :] + 1e-06)
+        ref, count = (qr0, NZ) if it == 0 else (qr1, 2 * NZ)
+        got(ref.at[pl.ds(0, count - 1)], phase(it, 7))
+        total = ref[0]
+        for k in range(1, count):
+            total = total + ref[k]
+        return jnp.sqrt(total + 1e-06)
 
     pl.semaphore_wait(barrier, len(greet))
     for d in NEAR_Z + [0]:
         for dc in (0, 1):
             if (d, dc) == (0, 0):
                 continue
-            to = along_z(d, dc)
+            to = near_z(d, dc)
             src = xs0.at[chunk(to[0] * 8 + lax.rem(to[2], 8), XCH)]
             put(src, xr0.at[0, pl.ds((2 * (d % 8) + dc) * XCH, XCH)], phase(0, 0), to)
     xr0[0, 0:XCH, :] = xs0[chunk(c * 8 + lax.rem(t, 8), XCH), :]
@@ -382,7 +388,7 @@
         xs1[0] = (0.5 * (acc[...] + products(0, 4))).astype(BF16)
 
     for d in NEAR_Z:
-        to = along_z(d)
+        to = near_z(d)
         src = xs1.at[0, chunk(lax.rem(to[2], 8), XCH)]
         put(src, xr1.at[0, pl.ds((d % 8) * XCH, XCH)], phase(1, 0), to)
     xr1[0, 0:XCH, :] = xs1[0, chunk(lax.rem(t, 8), XCH), :]
@@ -400,21 +406,40 @@
     right_out(1, left)
     xl[...] = left
     put(xl, xoth, 1, partner)
-    squares_send(0)
+    squares_send_core()
     gram_spread_all(gram_owned(1))
     right_spread(1)
     scale = jnp.broadcast_to(1.0 / norms(0), (RANK, RANK))
     a_s[...] = gram_join_all() * scale * scale.T
-    inverse_cholesky(a_s, lower.at[1], range(4))
+    inverse_cholesky(a_s, lower.at[1], range(8))
+    mix = lower[1] * scale
     right_join(1)
-    inverse_cholesky(a_s, lower.at[1], range(4, 8))
-    mix = lower[1] * scale
+
+    def right_tiles(first, last):
+        tiles = right_times(wa.at[1], mix, first, last)
+        for i in range(first, last):
+            right[i * 128 : (i + 1) * 128, :] = tiles[i - first]
+        return tiles
+
+    @pl.when(c == 0)
+    def _():
+        squares_sum(1, right_tiles(0, 4))
+
+    @pl.when(c == 1)
+    def _():
+        squares_sum(1, right_tiles(4, 7))
+
+    squares_send_all()
     right_here(1)
-    tiles = right_times(wa.at[1], mix)
-    squares_sum(1, tiles)
-    squares_send(1)
-    for i in range(TILES):
-        right[i * 128 : (i + 1) * 128, :] = tiles[i]
+
+    @pl.when(c == 0)
+    def _():
+        right_tiles(4, 7)
+
+    @pl.when(c == 1)
+    def _():
+        right_tiles(0, 4)
+
     got(xoth, 1)
     ob[mine, :] = rows_times(xl[...], mix).astype(BF16)
     ob[theirs, :] = rows_times(xoth[...], mix).astype(BF16)
@@ -424,35 +449,19 @@
         feedback = lax.dot_general(ob[r, :], right_b, nt, preferred_element_type=F32)
         new_mom[0, r, :] = (own[r, :].astype(F32) - 0.05 * feedback).astype(BF16)
 
-    sent(oth, 0)
-    sent(xl, 1)
-    sent(xr0.at[0, pl.ds(0, 15 * XCH)], phase(0, 0))
-    sent(xr1.at[0, pl.ds(0, 7 * XCH)], phase(1, 0))
-    sent(gp0.at[0, pl.ds(0, 15 * GCH)], phase(0, 6))
-    sent(ga.at[pl.ds(0, RANK // 2)], phase(0, 8))
-    sent(gp1.at[0, pl.ds(0, 31 * GCH)], phase(1, 6))
-    for it in range(2):
-        sent(xp.at[it, pl.ds(0, (NZ - 1) * XCH)], phase(it, 1))
-
-        @pl.when(owner)
-        def _():
-            sent(wr.at[it, pl.ds(0, 13 * WCH)], phase(it, 2))
-            sent(wr.at[it, pl.ds(0, 15 * WCH)], phase(it, 3))
-
-        @pl.when(idle)
-        def _():
-            sent(wr.at[it, pl.ds(0, 14 * WCH)], phase(it, 2))
-
-        @pl.when(c == 0)
-        def _():
-            sent(wa.at[it, pl.ds(0, 512)], phase(it, 4))
-
-        @pl.when(c == 1)
-        def _():
-            sent(wa.at[it, pl.ds(512, 384)], phase(it, 4))
-
-        sent(gr.at[it, pl.ds(0, 15 * GCH)], phase(it, 5))
-        sent(qr.at[it, pl.ds(0, (NZ - 1) * 8)], phase(it, 7))
+    everyone = 1792 + 256 + 480 + 224 + 2 * 480 + 2 * 240 + 240 + 496 + 128 + 30 + 62
+
+    @pl.when(c == 0)
+    def _():
+        all_sent(everyone + 2 * (13 * WCH + 15 * WCH + 512))
+
+    @pl.when((c == 1) & owner)
+    def _():
+        all_sent(everyone + 2 * (13 * WCH + 15 * WCH + 384))
+
+    @pl.when(idle)
+    def _():
+        all_sent(everyone + 2 * (14 * WCH + 384))
 
     norm[...] = jnp.broadcast_to(1.0 / norms(1), (8, RANK))
 
@@ -503,13 +512,15 @@
         pltpu.VMEM((1, 16 * GCH, RANK), F32),
         pltpu.VMEM((1, 32 * GCH, RANK), F32),
         pltpu.VMEM((RANK, RANK), F32),
-        pltpu.VMEM((2, 8, RANK), F32),
-        pltpu.VMEM((2, NZ * 8, RANK), F32),
+        pltpu.VMEM((2, 1, RANK), F32),
+        pltpu.VMEM((NZ, 1, RANK), F32),
+        pltpu.VMEM((2 * NZ, 1, RANK), F32),
         pltpu.VMEM((2, RANK, RANK), F32),
         pltpu.VMEM((RANK, RANK), F32),
         pltpu.VMEM((HALF, RANK), F32),
-        pltpu.SemaphoreType.DMA((9,)),
-        pltpu.SemaphoreType.DMA((20,)),
+        pltpu.VMEM((10400, RANK), BF16),
+        pltpu.SemaphoreType.DMA((5,)),
+        pltpu.SemaphoreType.DMA(()),
         pltpu.SemaphoreType.DMA((20,)),
     ]
     arguments = [

time: 78.9 us -> 77.8 us (0.986)
  Pallas kernels: 78 us -> 77 us
    pallas_call x1, Pallas kernels: 76.5 us -> 75.6 us  [shards(): pl.pallas_call(kernel, out_shape=(jax.ShapeDtypeStruct((1, ROWS, COLS), B...]
where the time goes in v5:
time: 77.8 us; the launch traced here: 77.7 us
  Pallas kernels  77 us (99%)
    pallas_call x1, Pallas kernels, shards(): pl.pallas_call(kernel, out_shape=(jax.ShapeDtypeStruct((1, ROWS, COLS), B...  75.6 us

profile of v5, /device:TPU:1, one launch (start us, length us, event | category | flops | bytes accessed | tf_op | source)
XLA Modules:
  0.0 77.7 jit_solution(11799609451956507315)
XLA Ops:
  0.6 75.6 %shard_map.58 = (bf16[1,512,896]{2,1,0:T(8,128)(2,1)S(1)}, f32[896,128]{1,0:T(8,128)S(1)}, bf16[512,128]{1,0:T(8,128)(2,1)S(1)}, f32[8,128]{1,0:T(8,128)S(1)}) custom-call(bf16[1,512,896]{2,1,0:T(8,128)(2,1)} %mom.1, bf16[1,512,896]{2,1,0:T(8,128)(2,1)} %grad.1, f32[896,128]{1,0:T(8,128)} %fac.1), custom_call_target="tpu_custom_call" | custom-call | flops 587202560 | bytes 4194304 | tf_op jit(solution)/shard_map/pallas_call | solution.py:532
  76.2 1.4 %shard_map.59 = (bf16[1,512,896]{2,1,0:T(8,128)(2,1)}, bf16[512,896]{1,0:T(8,128)(2,1)}, f32[896,128]{1,0:T(8,128)}) custom-call(bf16[1,512,896]{2,1,0:T(8,128)(2,1)S(1)} %get-tuple-element.7.new_mom, f32[896,128]{1,0:T(8,128)S(1)} %get-tuple-element.8.right, bf16[512,128]{1,0:T(8,128)(2,1)S(1)} %get-tuple-element.9.ob, f32[8,128]{1,0:T(8,128)S(1)} %get-tuple-element.10.norm), custom_call_target="tpu_custom_call" | custom-call | flops 117440512 | bytes 3145728 | tf_op jit(solution)/shard_map/pallas_call | solution.py:550

commit v6 on v5

--- a/solution.py
+++ b/solution.py
@@ -351,9 +351,9 @@
             src = xs0.at[chunk(to[0] * 8 + lax.rem(to[2], 8), XCH)]
             put(src, xr0.at[0, pl.ds((2 * (d % 8) + dc) * XCH, XCH)], phase(0, 0), to)
     xr0[0, 0:XCH, :] = xs0[chunk(c * 8 + lax.rem(t, 8), XCH), :]
-    put(own.at[theirs], oth, 0, partner)
     got(xr0.at[0, pl.ds(XCH, 15 * XCH)], phase(0, 0))
     left_spread(0, summed(xr0, 0, XCH, 16))
+    put(own.at[theirs], oth, 0, partner)
     got(oth, 0)
     left = left_here(0)
     right_out(0, left)
@@ -403,14 +403,15 @@
     squares_sum(0, right_times(wa.at[0], lower[0]))
     left = left_here(1)
     gram_out(1, left)
-    right_out(1, left)
+    squares_send_core()
     xl[...] = left
     put(xl, xoth, 1, partner)
-    squares_send_core()
+    right_out(1, left)
     gram_spread_all(gram_owned(1))
     right_spread(1)
     scale = jnp.broadcast_to(1.0 / norms(0), (RANK, RANK))
-    a_s[...] = gram_join_all() * scale * scale.T
+    a_s[...] = scale * scale.T
+    a_s[...] = gram_join_all() * a_s[...]
     inverse_cholesky(a_s, lower.at[1], range(8))
     mix = lower[1] * scale
     right_join(1)

time: 77.8 us -> 78 us (level)
  no operation moved by 1% of the time
where the time goes in v6:
time: 78 us; the launch traced here: 77.8 us
  Pallas kernels  77.2 us (99%)
    pallas_call x1, Pallas kernels, shards(): pl.pallas_call(kernel, out_shape=(jax.ShapeDtypeStruct((1, ROWS, COLS), B...  75.8 us

profile of v6, /device:TPU:1, one launch (start us, length us, event | category | flops | bytes accessed | tf_op | source)
XLA Modules:
  0.0 77.8 jit_solution(9011607503640144684)
XLA Ops:
  0.6 75.8 %shard_map.58 = (bf16[1,512,896]{2,1,0:T(8,128)(2,1)S(1)}, f32[896,128]{1,0:T(8,128)S(1)}, bf16[512,128]{1,0:T(8,128)(2,1)S(1)}, f32[8,128]{1,0:T(8,128)S(1)}) custom-call(bf16[1,512,896]{2,1,0:T(8,128)(2,1)} %mom.1, bf16[1,512,896]{2,1,0:T(8,128)(2,1)} %grad.1, f32[896,128]{1,0:T(8,128)} %fac.1), custom_call_target="tpu_custom_call" | custom-call | flops 587202560 | bytes 4194304 | tf_op jit(solution)/shard_map/pallas_call | solution.py:533
  76.4 1.4 %shard_map.59 = (bf16[1,512,896]{2,1,0:T(8,128)(2,1)}, bf16[512,896]{1,0:T(8,128)(2,1)}, f32[896,128]{1,0:T(8,128)}) custom-call(bf16[1,512,896]{2,1,0:T(8,128)(2,1)S(1)} %get-tuple-element.7.new_mom, f32[896,128]{1,0:T(8,128)S(1)} %get-tuple-element.8.right, bf16[512,128]{1,0:T(8,128)(2,1)S(1)} %get-tuple-element.9.ob, f32[8,128]{1,0:T(8,128)S(1)} %get-tuple-element.10.norm), custom_call_target="tpu_custom_call" | custom-call | flops 117440512 | bytes 3145728 | tf_op jit(solution)/shard_map/pallas_call | solution.py:551

commit v7 on v6

--- a/solution.py
+++ b/solution.py
@@ -141,22 +141,21 @@
     def chunk(index, size):
         return pl.ds(pl.multiple_of(index * size, size), size)
 
-    def put(src, dst, phase, to):
+    def put(src, dst, phase, to, group=0):
         pltpu.make_async_remote_copy(
-            src_ref=src, dst_ref=dst, send_sem=send, recv_sem=recv.at[phase],
+            src_ref=src, dst_ref=dst, send_sem=send.at[group], recv_sem=recv.at[phase],
             device_id=to, device_id_type=MESH,
         ).start()
 
     def got(region, phase):
         pltpu.make_async_remote_copy(
-            src_ref=region, dst_ref=region, send_sem=send, recv_sem=recv.at[phase],
+            src_ref=region, dst_ref=region, send_sem=send.at[0], recv_sem=recv.at[phase],
             device_id=partner, device_id_type=MESH,
         ).wait_recv()
 
-    def all_sent(rows):
-        region = tally.at[pl.ds(0, rows)]
+    def all_sent(region, group):
         pltpu.make_async_remote_copy(
-            src_ref=region, dst_ref=region, send_sem=send, recv_sem=recv.at[0],
+            src_ref=region, dst_ref=region, send_sem=send.at[group], recv_sem=recv.at[0],
             device_id=partner, device_id_type=MESH,
         ).wait_send()
 
@@ -323,15 +322,15 @@
 
     def squares_send_core():
         for to in ring:
-            put(qs.at[0], qr0.at[t], phase(0, 7), to)
+            put(qs.at[0], qr0.at[t], phase(0, 7), to, 1)
         qr0[t] = qs[0]
 
     def squares_send_all():
         slot = 2 * t + c
         for d in FAR_Z:
             for dc in (0, 1):
-                put(qs.at[1], qr1.at[slot], phase(1, 7), along_z(d, dc))
-        put(qs.at[1], qr1.at[slot], phase(1, 7), partner)
+                put(qs.at[1], qr1.at[slot], phase(1, 7), along_z(d, dc), 2)
+        put(qs.at[1], qr1.at[slot], phase(1, 7), partner, 2)
         qr1[slot] = qs[1]
 
     def norms(it):
@@ -450,19 +449,21 @@
         feedback = lax.dot_general(ob[r, :], right_b, nt, preferred_element_type=F32)
         new_mom[0, r, :] = (own[r, :].astype(F32) - 0.05 * feedback).astype(BF16)
 
-    everyone = 1792 + 256 + 480 + 224 + 2 * 480 + 2 * 240 + 240 + 496 + 128 + 30 + 62
+    all_sent(qr0.at[pl.ds(0, NZ - 1)], 1)
+    all_sent(qr1.at[pl.ds(0, 2 * NZ - 1)], 2)
+    everyone = 1792 + 256 + 480 + 224 + 2 * 480 + 2 * 240 + 240 + 496 + 128
 
     @pl.when(c == 0)
     def _():
-        all_sent(everyone + 2 * (13 * WCH + 15 * WCH + 512))
+        all_sent(tally.at[pl.ds(0, everyone + 2 * (13 * WCH + 15 * WCH + 512))], 0)
 
     @pl.when((c == 1) & owner)
     def _():
-        all_sent(everyone + 2 * (13 * WCH + 15 * WCH + 384))
+        all_sent(tally.at[pl.ds(0, everyone + 2 * (13 * WCH + 15 * WCH + 384))], 0)
 
     @pl.when(idle)
     def _():
-        all_sent(everyone + 2 * (14 * WCH + 384))
+        all_sent(tally.at[pl.ds(0, everyone + 2 * (14 * WCH + 384))], 0)
 
     norm[...] = jnp.broadcast_to(1.0 / norms(1), (8, RANK))
 
@@ -521,7 +522,7 @@
         pltpu.VMEM((HALF, RANK), F32),
         pltpu.VMEM((10400, RANK), BF16),
         pltpu.SemaphoreType.DMA((5,)),
-        pltpu.SemaphoreType.DMA(()),
+        pltpu.SemaphoreType.DMA((3,)),
         pltpu.SemaphoreType.DMA((20,)),
     ]
     arguments = [

time: 78 us -> 78 us (level)
  no operation moved by 1% of the time
where the time goes in v7:
time: 78 us; the launch traced here: 77.8 us
  Pallas kernels  77.2 us (99%)
    pallas_call x1, Pallas kernels, shards(): pl.pallas_call(kernel, out_shape=(jax.ShapeDtypeStruct((1, ROWS, COLS), B...  75.8 us

profile of v7, /device:TPU:1, one launch (start us, length us, event | category | flops | bytes accessed | tf_op | source)
XLA Modules:
  0.0 77.8 jit_solution(16389862229987414018)
XLA Ops:
  0.6 75.8 %shard_map.58 = (bf16[1,512,896]{2,1,0:T(8,128)(2,1)S(1)}, f32[896,128]{1,0:T(8,128)S(1)}, bf16[512,128]{1,0:T(8,128)(2,1)S(1)}, f32[8,128]{1,0:T(8,128)S(1)}) custom-call(bf16[1,512,896]{2,1,0:T(8,128)(2,1)} %mom.1, bf16[1,512,896]{2,1,0:T(8,128)(2,1)} %grad.1, f32[896,128]{1,0:T(8,128)} %fac.1), custom_call_target="tpu_custom_call" | custom-call | flops 587202560 | bytes 4194304 | tf_op jit(solution)/shard_map/pallas_call | solution.py:534
  76.4 1.4 %shard_map.59 = (bf16[1,512,896]{2,1,0:T(8,128)(2,1)}, bf16[512,896]{1,0:T(8,128)(2,1)}, f32[896,128]{1,0:T(8,128)}) custom-call(bf16[1,512,896]{2,1,0:T(8,128)(2,1)S(1)} %get-tuple-element.7.new_mom, f32[896,128]{1,0:T(8,128)S(1)} %get-tuple-element.8.right, bf16[512,128]{1,0:T(8,128)(2,1)S(1)} %get-tuple-element.9.ob, f32[8,128]{1,0:T(8,128)S(1)} %get-tuple-element.10.norm), custom_call_target="tpu_custom_call" | custom-call | flops 117440512 | bytes 3145728 | tf_op jit(solution)/shard_map/pallas_call | solution.py:552

commit v8 on v7

--- a/solution.py
+++ b/solution.py
@@ -400,16 +400,16 @@
     owned = jnp.concatenate([owned[0], owned[0], owned[1]], 1)
     left_spread(1, lax.dot_general(owned, low_parts, nt, preferred_element_type=F32))
     squares_sum(0, right_times(wa.at[0], lower[0]))
+    squares_send_core()
     left = left_here(1)
     gram_out(1, left)
-    squares_send_core()
     xl[...] = left
     put(xl, xoth, 1, partner)
     right_out(1, left)
+    scale = jnp.broadcast_to(1.0 / norms(0), (RANK, RANK))
+    a_s[...] = scale * scale.T
     gram_spread_all(gram_owned(1))
     right_spread(1)
-    scale = jnp.broadcast_to(1.0 / norms(0), (RANK, RANK))
-    a_s[...] = scale * scale.T
     a_s[...] = gram_join_all() * a_s[...]
     inverse_cholesky(a_s, lower.at[1], range(8))
     mix = lower[1] * scale

time: 78 us -> 77.5 us (level)
  no operation moved by 1% of the time
where the time goes in v8:
time: 77.5 us; the launch traced here: 77.4 us
  Pallas kernels  76.8 us (99%)
    pallas_call x1, Pallas kernels, shards(): pl.pallas_call(kernel, out_shape=(jax.ShapeDtypeStruct((1, ROWS, COLS), B...  75.3 us

profile of v8, /device:TPU:1, one launch (start us, length us, event | category | flops | bytes accessed | tf_op | source)
XLA Modules:
  0.0 77.4 jit_solution(726697621422039102)
XLA Ops:
  0.6 75.3 %shard_map.58 = (bf16[1,512,896]{2,1,0:T(8,128)(2,1)S(1)}, f32[896,128]{1,0:T(8,128)S(1)}, bf16[512,128]{1,0:T(8,128)(2,1)S(1)}, f32[8,128]{1,0:T(8,128)S(1)}) custom-call(bf16[1,512,896]{2,1,0:T(8,128)(2,1)} %mom.1, bf16[1,512,896]{2,1,0:T(8,128)(2,1)} %grad.1, f32[896,128]{1,0:T(8,128)} %fac.1), custom_call_target="tpu_custom_call" | custom-call | flops 587202560 | bytes 4194304 | tf_op jit(solution)/shard_map/pallas_call | solution.py:534
  76.0 1.4 %shard_map.59 = (bf16[1,512,896]{2,1,0:T(8,128)(2,1)}, bf16[512,896]{1,0:T(8,128)(2,1)}, f32[896,128]{1,0:T(8,128)}) custom-call(bf16[1,512,896]{2,1,0:T(8,128)(2,1)S(1)} %get-tuple-element.7.new_mom, f32[896,128]{1,0:T(8,128)S(1)} %get-tuple-element.8.right, bf16[512,128]{1,0:T(8,128)(2,1)S(1)} %get-tuple-element.9.ob, f32[8,128]{1,0:T(8,128)S(1)} %get-tuple-element.10.norm), custom_call_target="tpu_custom_call" | custom-call | flops 117440512 | bytes 3145728 | tf_op jit(solution)/shard_map/pallas_call | solution.py:552
